TPU v7x, 256 devices: a whole 4x4x8 slice. The times are simulated.
256 devices in a mesh: seq: 16 (over x, y), exp: 16 (over z, core).
Axes of the slice: x: 4, y: 4, z: 8, core: 2. Of those that a mesh axis runs over, the one named last changes fastest.
Arguments:
- tokens: bfloat16 [65536, 2048], P(('seq', 'exp')), may hold values from -6 to 6
- pick_rows: int32 [256, 48], P('seq'), may hold values from 0 to 255, as said below
- pick_counts: int32 [256], P('seq'), may hold values from 1 to 48, as said below
- expert_ids: int32 [12288, 6], P('seq'), may hold values from 0 to 15, all different within a row; in each aligned block of 48 rows (0 to 47, 48 to 95, ...) at most 26 rows name the same one
- norm_gains: float32 [2, 2048], replicated, may hold values from 0.5 to 1.5
- depth_router: bfloat16 [2048], replicated, may hold values from -0.125 to 0.125
- w_query: bfloat16 [2048, 2048], P(None, 'exp'), may hold values from -0.5 to 0.5
- w_keyval: bfloat16 [2, 2048, 2048], P(None, None, 'exp'), may hold values from -0.125 to 0.125
- w_out: bfloat16 [2048, 2048], P('exp'), may hold values from -0.125 to 0.125
- expert_router: bfloat16 [2048, 16], replicated, may hold values from -0.125 to 0.125
- w_expert: bfloat16 [16, 3, 2048, 1408], P('exp', None, None, 'seq'), may hold values from -0.125 to 0.125
Outputs:
- mixed: bfloat16 [65536, 2048], P(('seq', 'exp'))
- delta: float32 [12288, 2048], P(('seq', 'exp'))
Inputs may be any that keep to these rules, and one draw needn't show every extreme that they name: `pick_rows`: row d names rows of device d: its first pick_counts[d] entries are distinct and ascending, the picked tokens; the other entries are further distinct rows of that device and are not used. `pick_counts`: some device fills all of its 48 slots. `expert_ids`: the 6 experts of a slot are distinct; within the 48 slots of one device (aligned blocks of rows) no expert is named more than 26 times, counting unused slots too.
All inputs are finite; a program needn't handle non-finite values.
Results may differ from a plain program's by a relative error of at most 0.023.
Values may be sent and summed in bfloat16 or wider, within the bound.
A program may use at most 128 MiB of HBM per device.

v0:
```python
import jax
import jax.numpy as jnp
from jax import lax
from jax.sharding import PartitionSpec as P

HEAD_DIM = 128


far_position = 1 << 30
softcap_limit = 20.0


def normalize(values, gain):
    widened = values.astype(jnp.float32)
    scale = lax.rsqrt(jnp.mean(widened * widened, axis=-1, keepdims=True) + 1e-06)
    return (widened * scale * gain).astype(jnp.bfloat16)


def soft_limit(scores):
    return softcap_limit * jnp.tanh(scores / softcap_limit)


def expert_apply(inputs, local_weights):
    matrices = lax.all_gather(local_weights, "seq", axis=3, tiled=True)[0]
    gated = jnp.dot(inputs, matrices[0], preferred_element_type=jnp.float32)
    upward = jnp.dot(inputs, matrices[1], preferred_element_type=jnp.float32)
    hidden = (jax.nn.silu(gated) * upward).astype(jnp.bfloat16)
    result = lax.dot_general(
        hidden, matrices[2], (((1,), (1,)), ((), ())), preferred_element_type=jnp.float32
    )
    return result.astype(jnp.bfloat16)


def route_weights(normed, router, chosen_ids):
    scores = jax.nn.sigmoid(jnp.dot(normed, router, preferred_element_type=jnp.float32))
    onehot = chosen_ids[:, :, None] == jnp.arange(router.shape[1], dtype=jnp.int32)[None, None, :]
    picked_scores = jnp.sum(jnp.where(onehot, scores[:, None, :], jnp.float32(0.0)), axis=-1)
    return picked_scores / jnp.sum(picked_scores, axis=-1, keepdims=True)


def slot_numbers(chosen_ids, valid, experts):
    onehot = (
        (chosen_ids[:, :, None] == jnp.arange(experts, dtype=jnp.int32)[None, None, :])
        & valid[:, None, None]
    ).astype(jnp.int32)
    flat = onehot.reshape(-1, experts)
    before = jnp.cumsum(flat, axis=0) - flat
    return jnp.sum(before * flat, axis=-1).reshape(chosen_ids.shape)


def local(
    tokens,
    pick_rows,
    pick_counts,
    expert_ids,
    norm_gains,
    depth_router,
    w_query,
    w_keyval,
    w_out,
    expert_router,
    w_expert,
):
    exp_count = lax.axis_size("exp")
    seq_place = lax.axis_index("seq")
    exp_place = lax.axis_index("exp")
    tok_rows = tokens.shape[0]
    width = tokens.shape[1]
    pick_slots = pick_rows.shape[1]
    head_cols = w_query.shape[1]
    heads_here = head_cols // HEAD_DIM
    experts = w_expert.shape[0] * exp_count
    top_count = expert_ids.shape[1]
    capacity = min(pick_slots, pick_slots * top_count // experts + 8)
    group_size = exp_count * pick_slots
    scale = HEAD_DIM ** (-0.5)
    slot_range = jnp.arange(pick_slots, dtype=jnp.int32)
    group_valid = slot_range[None, :] < pick_counts[:, None]
    device_ids = seq_place * exp_count + jnp.arange(exp_count, dtype=jnp.int32)
    group_pos = jnp.where(
        group_valid, device_ids[:, None] * tok_rows + pick_rows, far_position
    ).reshape(-1)
    key_rank = far_position - group_pos
    threshold = far_position - group_pos
    my_rows = lax.dynamic_index_in_dim(pick_rows, exp_place, 0, keepdims=False)
    my_valid = lax.dynamic_index_in_dim(group_valid, exp_place, 0, keepdims=False)
    my_ids = lax.dynamic_slice_in_dim(expert_ids, exp_place * pick_slots, pick_slots, 0)
    picked = tokens[my_rows]
    normed = normalize(lax.all_gather(picked, "exp", axis=0, tiled=True), norm_gains[0])
    query_part = jnp.dot(normed, w_query, preferred_element_type=jnp.float32).astype(jnp.bfloat16)
    key_part = jnp.dot(normed, w_keyval[0], preferred_element_type=jnp.float32).astype(jnp.bfloat16)
    value_part = jnp.dot(normed, w_keyval[1], preferred_element_type=jnp.float32).astype(
        jnp.bfloat16
    )
    projected = jnp.concatenate([query_part, key_part, value_part], axis=1)
    queries = projected[:, :head_cols].reshape(group_size, heads_here, HEAD_DIM)
    keyval = projected[:, head_cols:]
    piece_kv = lax.all_gather(keyval, "seq", axis=0, tiled=True)
    piece_rank = lax.all_gather(key_rank, "seq", axis=0, tiled=True)
    piece_rows = piece_kv.shape[0]
    piece_keys = piece_kv[:, :head_cols].reshape(piece_rows, heads_here, HEAD_DIM)
    piece_values = piece_kv[:, head_cols:].reshape(piece_rows, heads_here, HEAD_DIM)
    scores = (
        jnp.einsum("qhd,khd->hqk", queries, piece_keys, preferred_element_type=jnp.float32) * scale
    )
    allowed = piece_rank[None, None, :] >= threshold[None, :, None]
    weight = jnp.where(allowed, jnp.exp(soft_limit(scores)), jnp.float32(0.0))
    mass = jnp.sum(weight, axis=-1)
    total = jnp.einsum(
        "hqk,khd->qhd",
        weight.astype(jnp.bfloat16),
        piece_values,
        preferred_element_type=jnp.float32,
    )
    folded = (total, mass)
    total, mass = folded
    safe_mass = jnp.where(mass > 0, mass, jnp.float32(1.0))
    attended = (
        (total / jnp.transpose(safe_mass)[:, :, None])
        .astype(jnp.bfloat16)
        .reshape(group_size, head_cols)
    )
    head_mine = lax.psum_scatter(
        jnp.dot(attended, w_out, preferred_element_type=jnp.float32).astype(jnp.bfloat16),
        "exp",
        scatter_dimension=0,
        tiled=True,
    ).astype(jnp.float32)
    normed_mine = normalize(picked.astype(jnp.float32) + head_mine, norm_gains[1])
    shares = route_weights(normed_mine, expert_router, my_ids)
    slots = slot_numbers(my_ids, my_valid, experts)
    target = my_ids * capacity + slots
    placing = (
        target[:, :, None] == jnp.arange(experts * capacity, dtype=jnp.int32)[None, None, :]
    ) & my_valid[:, None, None]
    dispatch_table = jnp.sum(placing.astype(jnp.int32), axis=1).astype(jnp.bfloat16)
    outgoing = lax.dot_general(
        dispatch_table, normed_mine, (((0,), (0,)), ((), ())), preferred_element_type=jnp.float32
    )
    outgoing = outgoing.astype(jnp.bfloat16).reshape(experts, capacity, width)
    arrived = lax.all_to_all(outgoing, "exp", split_axis=0, concat_axis=0, tiled=True)
    served = expert_apply(arrived.reshape(-1, width), w_expert).reshape(arrived.shape)
    returned = lax.all_to_all(served, "exp", split_axis=0, concat_axis=0, tiled=True)
    lookup = jnp.where(my_valid[:, None], target, 0)
    pulled = returned.reshape(experts * capacity, width)[lookup]
    live_shares = jnp.where(my_valid[:, None], shares, jnp.float32(0.0))
    mixture = jnp.sum(live_shares[:, :, None] * pulled.astype(jnp.float32), axis=1)
    delta = jnp.where(my_valid[:, None], head_mine + mixture, jnp.float32(0.0))
    gate = jax.nn.sigmoid(jnp.dot(picked, depth_router, preferred_element_type=jnp.float32))
    update = jnp.where(my_valid[:, None], gate[:, None] * delta, jnp.float32(0.0))
    mixed = tokens.astype(jnp.float32).at[my_rows].add(update).astype(jnp.bfloat16)
    return (mixed, delta)


def solution(mesh):
    in_specs = (
        P(("seq", "exp"), None),
        P("seq", None),
        P("seq"),
        P("seq", None),
        P(),
        P(),
        P(None, "exp"),
        P(None, None, "exp"),
        P("exp", None),
        P(),
        P("exp", None, None, "seq"),
    )
    out_specs = (P(("seq", "exp"), None), P(("seq", "exp"), None))
    return jax.shard_map(local, mesh=mesh, in_specs=in_specs, out_specs=out_specs, check_vma=False)
```

profile of v0, /device:TPU:1, one launch (start us, length us, event | category | flops | bytes accessed | tf_op | source)
XLA Modules:
  0.0 446.7 jit_solution(17096543244524707978)
XLA Ops:
  7.2 0.0 all-gather.10.cloned.1.call-start
  7.2 0.7 fusion.67
  8.0 2.9 gather_fusion
  10.9 0.0 all-gather.10.cloned.1.call-update
  10.9 0.0 all-gather.6.cloned.1.call-start
  11.0 0.8 fusion.75
  11.8 44.5 %all-gather.10.cloned.1.call-done = bf16[768,2048]{1,0:T(8,128)(2,1)} async-done(((bf16[48,2048]{1,0:T(8,128)(2,1)}), bf16[768,2048]{1,0:T(8,128)(2,1)}) %all-gather.10.cloned.1.call-update) | async-done | bytes 3145744 | tf_op jit(solution)/shard_map/all_gather | solution.py:89
  56.3 2.7 fusion.4
  59.0 0.1 copy-done.3
  59.1 0.8 fusion.6
  59.9 0.4 copy-done.10
  60.3 1.2 convolution_convert_fusion.3
  61.5 1.2 convolution_convert_fusion.4
  62.7 0.8 pad_maximum_fusion
  63.5 0.0 all-gather.6.cloned.1.call-update
  63.5 0.0 reduce-scatter.2.cloned.1.call-start
  63.6 0.1 select_subtract_fusion
  63.7 0.1 reshape.220
  63.8 0.1 sub.15
  63.9 18.7 %all-gather.1 = s32[16,1,768]{2,1,0:T(1,128)S(1)} all-gather(s32[1,1,768]{2,1,0:T(1,128)S(1)} %reshape.220), channel_id=1, replica_groups=mesh['seq'=16,'exp'=16] {'seq'}, dimensions={0}, use_global_device_ids=true | all-gather | bytes 52224 | tf_op jit(solution)/shard_map/all_gather | solution.py:99
  82.5 45.6 %all-gather.6.cloned.1.call-done = bf16[12288,256]{0,1:T(8,128)(2,1)} async-done(((bf16[768,256]{0,1:T(8,128)(2,1)}), bf16[12288,256]{0,1:T(8,128)(2,1)}) %all-gather.6.cloned.1.call-update) | async-done | bytes 6291472 | tf_op jit(solution)/shard_map/all_gather | solution.py:98
  128.2 20.4 %fusion = (f32[768]{0:T(1024)S(1)}, f32[768,12288]{1,0:T(8,128)}) fusion(s32[12288]{0:T(1024)S(1)} %bitcast.85, s32[768]{0:T(1024)S(1)} %sub.15, bf16[12288,256]{0,1:T(8,128)(2,1)} %all-gather.6.cloned.1.call-done, bf16[768,2048]{1,0:T(8,128)(2,1)} %copy-done.2, bf16[2048,128]{1,0:T(8,128)(2,1)S(1)} %copy-done), kind=kOutput, calls=%fused_computation.4 | convolution fusion | flops 2865855744 | bytes 44619776 | tf_op jit(solution)/shard_map/qhd,khd->hqk/dot_general | solution.py:104
  148.6 19.9 %convolution_convert_fusion = bf16[768,2048]{1,0:T(8,128)(2,1)} fusion(bf16[128,2048]{1,0:T(8,128)(2,1)S(1)} %copy-done.14, f32[768,12288]{1,0:T(8,128)} %get-tuple-element.9, s32[12288]{0:T(1024)S(1)} %bitcast.86, s32[768]{0:T(1024)S(1)} %sub.15, bf16[12288,256]{0,1:T(8,128)(2,1)} %all-gather.6.cloned.1.call-done, f32[768]{0:T(1024)S(1)} %compare_select_fusion.1), kind=kOutput, calls=%fused_computation.18 | convolution fusion | flops 2867527680 | bytes 44619776 | tf_op jit(solution)/shard_map/dot_general | solution.py:124
  168.5 0.0 all-gather.8.cloned.1.call-start
  168.6 0.5 all-gather.8.cloned.1.call-update
  169.1 0.8 constant_dynamic-slice_fusion
  169.9 0.1 copy.26
  170.0 0.1 eq.52
  170.1 0.1 iota_compare_fusion.4
  170.2 0.1 broadcast_in_dim.94.clone
  170.3 0.1 and.26
  170.4 0.9 reduce-window.6
  171.3 0.2 slice_reduce_fusion
  171.6 0.1 bitcast_bitcast_fusion
  171.7 0.1 reshape.186
  171.8 0.1 copy.30
  171.9 0.8 compare_select_fusion
  172.7 0.1 convert_reduce_fusion
  172.8 53.6 %reduce-scatter.2.cloned.1.call-done = bf16[48,2048]{1,0:T(8,128)(2,1)} async-done(((bf16[768,2048]{1,0:T(8,128)(2,1)}), bf16[48,2048]{1,0:T(8,128)(2,1)}) %reduce-scatter.2.cloned.1.call-update) | async-done | bytes 196624 | tf_op jit(solution)/shard_map/reduce_scatter | solution.py:123
  226.4 1.1 multiply_reduce_fusion.1
  227.5 2.8 convolution_convert_fusion.1
  230.3 1.7 reshape.187
  232.0 58.9 %all_to_all.10 = bf16[16,26,2048]{2,1,0:T(8,128)(2,1)} all-to-all(bf16[16,26,2048]{2,1,0:T(8,128)(2,1)S(1)} %reshape.187), channel_id=1, replica_groups=mesh['seq'=16,'exp'=16] {'exp'}, dimensions={0} | all-to-all | bytes 3407872 | tf_op jit(solution)/shard_map/all_to_all | solution.py:141
  290.9 1.8 reshape.188
  292.7 56.5 %all-gather.8.cloned.1.call-done = bf16[1,3,2048,1408]{2,3,1,0:T(8,128)(2,1)} async-done(((bf16[1,3,2048,88]{2,3,1,0:T(8,128)(2,1)}), bf16[1,3,2048,1408]{2,3,1,0:T(8,128)(2,1)}) %all-gather.8.cloned.1.call-update) | async-done | bytes 17301520 | tf_op jit(solution)/shard_map/all_gather | solution.py:24
  349.2 6.9 %fusion.9 = f32[416,1408]{1,0:T(8,128)} fusion(bf16[416,2048]{1,0:T(8,128)(2,1)S(1)} %reshape.188, bf16[1,3,2048,1408]{2,3,1,0:T(8,128)(2,1)} %all-gather.8.cloned.1.call-done), kind=kOutput, calls=%fused_computation.17 | convolution fusion | flops 2399141888 | bytes 9814016 | tf_op jit(solution)/shard_map/dot_general | solution.py:25
  356.1 11.7 %fusion.15 = bf16[416,2048]{1,0:T(8,128)(2,1)} fusion(bf16[1,3,2048,1408]{2,3,1,0:T(8,128)(2,1)} %all-gather.8.cloned.1.call-done, bf16[416,2048]{1,0:T(8,128)(2,1)S(1)} %reshape.188, f32[416,1408]{1,0:T(8,128)} %fusion.9), kind=kOutput, calls=%fused_computation.26 | convolution fusion | flops 4802650112 | bytes 17285120 | tf_op jit(solution)/shard_map/dot_general | solution.py:28
  367.9 2.8 reshape.189
  370.7 7.8 %all-to-all-start.1 = ((bf16[16,26,2048]{2,1,0:T(8,128)(2,1)}), bf16[16,26,2048]{2,1,0:T(8,128)(2,1)}, u32[]{:S(2)}, u32[]{:S(2)}) async-start(bf16[16,26,2048]{2,1,0:T(8,128)(2,1)} %reshape.189), calls=%async_computation.2 | async-start | bytes 4194304 | tf_op jit(solution)/shard_map/all_to_all | solution.py:143
  378.6 1.6 convert_element_type.66
  380.2 0.1 copy.31
  380.3 0.1 reshape.202
  380.4 0.2 fusion.28
  380.6 0.2 fusion.24
  380.8 0.1 select_reduce_fusion
  380.9 0.1 copy.25
  381.0 46.6 %all-to-all-done.1 = bf16[16,26,2048]{2,1,0:T(8,128)(2,1)} async-done(((bf16[16,26,2048]{2,1,0:T(8,128)(2,1)}), bf16[16,26,2048]{2,1,0:T(8,128)(2,1)}, u32[]{:S(2)}, u32[]{:S(2)}) %all-to-all-start.1) | async-done | bytes 1703968 | tf_op jit(solution)/shard_map/all_to_all | solution.py:143
  427.6 1.8 reshape.190
  429.4 2.4 gather_fusion.1
  431.9 1.8 reshape.219
  433.7 3.2 multiply_reduce_fusion
  436.9 0.1 fusion.53
  437.0 2.1 scatter_custom_fusion
  439.1 1.1 convert_element_type.86
  (44 shorter events, 0.2 us)
Async XLA Ops:
  7.2 121.0 %copy-start = (bf16[2048,128]{1,0:T(8,128)(2,1)S(1)}, bf16[2048,128]{1,0:T(8,128)(2,1)}, u32[]{:S(2)}) copy-start(bf16[2048,128]{1,0:T(8,128)(2,1)} %param.17) | copy-start | bytes 1572868
  7.2 49.1 %all-gather.10.cloned.1.call-start = ((), (), s32[]{:S(2)}) async-start(), calls=%async_computation.6 | async-start | bytes 3342336 | tf_op jit(solution)/shard_map/all_gather | solution.py:89
  10.9 117.3 %all-gather.6.cloned.1.call-start = ((), (), s32[]{:S(2)}) async-start(), calls=%async_computation.3 | async-start | bytes 6684672 | tf_op jit(solution)/shard_map/all_gather | solution.py:98
  56.3 2.8 copy-start.3
  59.1 1.2 copy-start.10
  60.3 2.4 copy-start.2
  61.5 2.1 copy-start.11
  61.5 2.1 copy-start.13
  63.5 162.9 %reduce-scatter.2.cloned.1.call-start = ((), (), s32[]{:S(2)}) async-start(), calls=%async_computation.4 | async-start | bytes 3342336 | tf_op jit(solution)/shard_map/reduce_scatter | solution.py:123
  128.2 20.4 %copy-start.14 = (bf16[128,2048]{1,0:T(8,128)(2,1)S(1)}, bf16[128,2048]{1,0:T(8,128)(2,1)}, u32[]{:S(2)}) copy-start(bf16[128,2048]{1,0:T(8,128)(2,1)} %param.19) | copy-start | bytes 1572868
  168.5 57.9 %copy-start.6 = (bf16[48,2048]{1,0:T(8,128)(2,1)S(1)}, bf16[48,2048]{1,0:T(8,128)(2,1)}, u32[]{:S(2)}) copy-start(bf16[48,2048]{1,0:T(8,128)(2,1)} %gather_fusion) | copy-start | bytes 589828
  168.5 180.7 %all-gather.8.cloned.1.call-start = ((), (), s32[]{:S(2)}) async-start(), calls=%async_computation.5 | async-start | bytes 18382848 | tf_op jit(solution)/shard_map/all_gather | solution.py:24
  367.9 10.7 %copy-start.5 = (bf16[256,2048]{1,0:T(8,128)(2,1)S(1)}, bf16[256,2048]{1,0:T(8,128)(2,1)}, u32[]{:S(2)}) copy-start(bf16[256,2048]{1,0:T(8,128)(2,1)} %param.11) | copy-start | bytes 3145732
  370.7 9.7 %copy-start.12 = (bf16[2048]{0:T(1024)(128)(2,1)S(1)}, bf16[2048]{0:T(1024)(128)(2,1)}, u32[]{:S(2)}) copy-start(bf16[2048]{0:T(1024)(128)(2,1)} %param.16) | copy-start | bytes 12292
  370.7 9.9 %copy-start.7 = (bf16[48,2048]{1,0:T(8,128)(2,1)S(1)}, bf16[48,2048]{1,0:T(8,128)(2,1)}, u32[]{:S(2)}) copy-start(bf16[48,2048]{1,0:T(8,128)(2,1)} %reduce-scatter.2.cloned.1.call-done) | copy-start | bytes 589828
  370.7 9.9 %copy-start.15 = (bf16[2048,16]{0,1:T(8,128)(2,1)S(1)}, bf16[2048,16]{0,1:T(8,128)(2,1)}, u32[]{:S(2)}) copy-start(bf16[2048,16]{0,1:T(8,128)(2,1)} %param.20) | copy-start | bytes 196612
  370.7 56.9 %all-to-all-start.1 = ((bf16[16,26,2048]{2,1,0:T(8,128)(2,1)}), bf16[16,26,2048]{2,1,0:T(8,128)(2,1)}, u32[]{:S(2)}, u32[]{:S(2)}) async-start(bf16[16,26,2048]{2,1,0:T(8,128)(2,1)} %reshape.189), calls=%async_computation.2 | async-start | bytes 4194304 | tf_op jit(solution)/shard_map/all_to_all | solution.py:143
  433.7 3.2 copy-start.8
  433.7 3.3 copy-start.4
  433.7 6.5 %copy-start.1 = (bf16[2048,128]{1,0:T(8,128)(2,1)S(1)}, bf16[2048,128]{1,0:T(8,128)(2,1)}, u32[]{:S(2)}) copy-start(bf16[2048,128]{1,0:T(8,128)(2,1)} %param.17) | copy-start | bytes 1572868
  437.0 3.2 copy-start.9
Sparse Core Ops, SparseCore 0:
  11.0 45.1 all-gather.9
  63.6 64.4 all-gather.5
  168.7 57.6 reduce-scatter.1
  228.7 120.5 all-gather.7
where the time goes:
time: 447 us
  waiting for transfers between devices  247 us (55%)
  blocking collectives  77.5 us (17%)
  matrix products  64.5 us (14%)
  local copies, waits for them, and re-layouts  18.8 us (4%)
  other arithmetic  16.4 us (4%)
  between operations  14 us (3%)
  starting transfers between devices  8 us (2%)
    all_to_all x1, blocking collectives, local(): lax.all_to_all(outgoing, 'exp', split_axis=0, concat_axis=0, tiled=True)  58.9 us
    all_gather x1, waiting for transfers between devices, expert_apply(): matrices = lax.all_gather(local_weights, 'seq', axis=3, tiled=True)[0]  56.5 us
    reduce_scatter x1, waiting for transfers between devices, local(): lax.psum_scatter(jnp.dot(attended, w_out, preferred_element_type=jnp.floa...  53.6 us
    all_to_all x1, waiting for transfers between devices, local(): lax.all_to_all(served, 'exp', split_axis=0, concat_axis=0, tiled=True)  46.6 us
    all_gather x1, waiting for transfers between devices, local(): piece_kv = lax.all_gather(keyval, 'seq', axis=0, tiled=True)  45.6 us
    all_gather x1, waiting for transfers between devices, local(): lax.all_gather(picked, 'exp', axis=0, tiled=True)  44.5 us
    dot_general x1, matrix products, local(): jnp.einsum('qhd,khd->hqk', queries, piece_keys, preferred_element_type=jn...  20.4 us
    dot_general x1, matrix products, local(): jnp.dot(attended, w_out, preferred_element_type=jnp.float32)  19.9 us
  transfers between devices with their start and end apart: 5, of which 5 were waited for; matrix products, arithmetic and copies ran while one was open for 3% of the time, Pallas kernels for 0%

commit v1 on v0

v1 whole, which is shorter than its diff:
```python
import functools
import math

import jax
import jax.numpy as jnp
from jax import lax
from jax.experimental import pallas as pl
from jax.experimental.pallas import tpu as pltpu
from jax.sharding import PartitionSpec as P

HEAD_DIM = 128
softcap_limit = 20.0
MESH = pl.DeviceIdType.MESH
SIDE = 4
RING = 8
SLOTS = 48
SHARD = 768
WIDTH = 2048
HALF = 1024
QUARTER = 192
VMEM = pl.BlockSpec(memory_space=pltpu.VMEM)


def wrap(value, size):
    return lax.rem(value + size, size)


def hops(direction, half):
    return 4 if (direction > 0) == (half == 0) else 3


def hop_number(direction, half, hop):
    return ((0 if direction > 0 else 1) * 2 + half) * 4 + hop - 1


def at_exp(index):
    return {"exp": index}


def ring_place():
    place = lax.axis_index("exp")
    return lax.div(place, 2), lax.rem(place, 2)


def greet(partners):
    barrier = pltpu.get_barrier_semaphore()
    for partner in partners:
        pl.semaphore_signal(barrier, inc=1, device_id=partner, device_id_type=MESH)
    pl.semaphore_wait(barrier, len(partners))


def ring_partners():
    z, core = ring_place()
    return [
        at_exp(2 * wrap(z + 1, RING) + core),
        at_exp(2 * wrap(z - 1, RING) + core),
        at_exp(2 * z + 1 - core),
    ]


def remote(src, dst, send, recv, target):
    return pltpu.make_async_remote_copy(
        src_ref=src, dst_ref=dst, send_sem=send, recv_sem=recv, device_id=target, device_id_type=MESH
    )


def ring_gather(buf, send, recv, sib_send, sib_recv):
    z, core = ring_place()
    sibling = at_exp(2 * z + 1 - core)

    def part(origin, side, half):
        return buf.at[2 * origin + side, :, pl.ds(half * HALF, HALF)]

    def hop_copy(direction, half, hop, arriving):
        origin = wrap(z - direction * (hop if arriving else hop - 1), RING)
        ref = part(origin, core, half)
        number = hop_number(direction, half, hop)
        return remote(ref, ref, send.at[number], recv.at[number], at_exp(2 * wrap(z + direction, RING) + core))

    def sib_copy(direction, half, hop, arriving):
        origin = wrap(z - direction * hop, RING)
        ref = part(origin, 1 - core if arriving else core, half)
        number = hop_number(direction, half, hop)
        return remote(ref, ref, sib_send.at[number], sib_recv.at[number], sibling)

    def own_copy(arriving):
        ref = buf.at[2 * z + (1 - core if arriving else core)]
        return remote(ref, ref, sib_send.at[16], sib_recv.at[16], sibling)

    lanes = [(1, 0), (-1, 1), (1, 1), (-1, 0)]
    for direction, half in lanes:
        hop_copy(direction, half, 1, False).start()
    own_copy(False).start()
    for hop in range(1, 5):
        for direction, half in lanes:
            if hop <= hops(direction, half):
                hop_copy(direction, half, hop, True).wait_recv()
                if hop < hops(direction, half):
                    hop_copy(direction, half, hop + 1, False).start()
                sib_copy(direction, half, hop, False).start()
    own_copy(True).wait_recv()
    own_copy(False).wait_send()
    for hop in range(1, 5):
        for direction, half in lanes:
            if hop <= hops(direction, half):
                sib_copy(direction, half, hop, True).wait_recv()
                sib_copy(direction, half, hop, False).wait_send()
                hop_copy(direction, half, hop, False).wait_send()


def ring_scatter(part, sib, out_buf, in_buf, total, send, recv, sib_send, sib_recv):
    z, core = ring_place()
    sibling = at_exp(2 * z + 1 - core)

    def sib_copy(offset):
        target = wrap(z + offset, RING)
        return remote(
            part.at[2 * target + 1 - core], sib.at[target], sib_send.at[offset % RING], sib_recv.at[offset % RING], sibling
        )

    def mine(target, half):
        columns = pl.ds(half * HALF, HALF)
        return part[2 * target + core, :, columns].astype(jnp.float32) + sib[target, :, columns].astype(jnp.float32)

    def hop_copy(direction, half, hop):
        number = hop_number(direction, half, hop)
        return remote(
            out_buf.at[number], in_buf.at[number], send.at[number], recv.at[number],
            at_exp(2 * wrap(z + direction, RING) + core),
        )

    order = [4, 3, -3, 2, -2, 1, -1, 0]
    for offset in order:
        sib_copy(offset).start()
    arrived = set()
    lanes = [(1, 0), (-1, 1), (1, 1), (-1, 0)]

    def have(offset):
        if offset % RING not in arrived:
            arrived.add(offset % RING)
            sib_copy(offset).wait_recv()

    for hop in range(1, 5):
        for direction, half in lanes:
            last = hops(direction, half)
            if hop <= last:
                offset = direction * (last - hop + 1)
                have(offset)
                number = hop_number(direction, half, hop)
                value = mine(wrap(z + offset, RING), half)
                if hop > 1:
                    hop_copy(direction, half, hop - 1).wait_recv()
                    value = value + in_buf[number - 1].astype(jnp.float32)
                out_buf[number] = value.astype(jnp.bfloat16)
                hop_copy(direction, half, hop).start()
    have(0)
    for half in range(2):
        value = mine(z, half)
        for direction in (1, -1):
            last = hops(direction, half)
            hop_copy(direction, half, last).wait_recv()
            value = value + in_buf[hop_number(direction, half, last)].astype(jnp.float32)
        total[:, half * HALF : (half + 1) * HALF] = value
    for offset in order:
        sib_copy(offset).wait_send()
    for direction, half in lanes:
        for hop in range(1, hops(direction, half) + 1):
            hop_copy(direction, half, hop).wait_send()


def normalize(widened, gain):
    scale = lax.rsqrt(jnp.mean(widened * widened, axis=-1, keepdims=True) + 1e-06)
    return (widened * scale * gain).astype(jnp.bfloat16)


def live_lanes(counts):
    row = lax.broadcasted_iota(jnp.int32, (SHARD, 16), 0)
    first = lax.broadcasted_iota(jnp.int32, (SHARD, 16), 1) * SLOTS
    spread = jnp.where((row >= first) & (row < first + SLOTS), 1.0, 0.0).astype(jnp.bfloat16)
    block = lax.broadcasted_iota(jnp.int32, (16, 128), 0).astype(jnp.float32)
    count_of = jnp.dot(spread, counts.astype(jnp.bfloat16), preferred_element_type=jnp.float32)
    block_of = jnp.dot(spread, block.astype(jnp.bfloat16), preferred_element_type=jnp.float32)
    slot = lax.broadcasted_iota(jnp.int32, (SHARD, 128), 0).astype(jnp.float32) - block_of * SLOTS
    return jnp.where(slot < count_of, 1.0, 0.0)


def project_kernel(
    tokens, rows, counts, gains, w_query, w_keyval, picked, queries, keyval, buf, send, recv, sib_send, sib_recv
):
    place = lax.axis_index("exp")
    greet(ring_partners())
    mine = rows[pl.ds(place, 1), :]
    onehot = jnp.where(
        lax.broadcasted_iota(jnp.int32, (tokens.shape[0], SLOTS), 0) == mine, 1.0, 0.0
    ).T.astype(jnp.bfloat16)
    chosen = jnp.dot(onehot, tokens[...], preferred_element_type=jnp.float32)
    picked[...] = chosen.astype(jnp.bfloat16)
    buf[place] = normalize(chosen, gains[0:1, :])
    ring_gather(buf, send, recv, sib_send, sib_recv)
    normed = buf[...].reshape(SHARD, WIDTH)
    queries[...] = jnp.dot(normed, w_query[...], preferred_element_type=jnp.float32).astype(jnp.bfloat16)
    keys = jnp.dot(normed, w_keyval[0], preferred_element_type=jnp.float32).astype(jnp.bfloat16)
    values = jnp.dot(normed, w_keyval[1], preferred_element_type=jnp.float32)
    values = (values * live_lanes(counts[...])).astype(jnp.bfloat16)
    keyval[:, :, 0:HEAD_DIM] = keys.reshape(4, QUARTER, HEAD_DIM)
    keyval[:, :, HEAD_DIM:] = values.reshape(4, QUARTER, HEAD_DIM)


def torus_place():
    place = lax.axis_index("seq")
    return lax.div(place, SIDE), lax.rem(place, SIDE)


def attend_kernel(
    queries, keyval, counts, w_out, part, kv, tallies, acc, send, recv, count_send, count_recv
):
    x, y = torus_place()
    seq = lax.axis_index("seq")

    def at(px, py):
        return {"seq": wrap(px, SIDE) * SIDE + wrap(py, SIDE)}

    greet(
        [at(x, y + 1), at(x, y - 1), at(x, y + 2), at(x + 1, y), at(x - 1, y), at(x + 2, y)]
    )

    def shifted(quarter, first, second):
        if quarter < 2:
            return x + second, y + first
        return x + first, y + second

    def slot(quarter, first, second):
        px, py = shifted(quarter, first, second)
        return wrap(px, SIDE) * SIDE + wrap(py, SIDE)

    def flow(quarter):
        return 1 if quarter % 2 == 0 else -1

    def lines(quarter):
        d = flow(quarter)
        return [0, -d, d, -2 * d]

    def arriving(quarter, number):
        d = flow(quarter)
        if number < 3:
            return [(-d, 0), (d, 0), (-2 * d, 0)][number]
        line, kind = divmod(number - 3, 3)
        return lines(quarter)[line], [-d, d, -2 * d][kind]

    def copy(quarter, number, incoming):
        first, second = arriving(quarter, number)
        d = flow(quarter)
        kind = number if number < 3 else (number - 3) % 3
        step = d if kind in (0, 2) else -d
        if not incoming:
            if number < 3:
                first = first + step
            else:
                second = second + step
        ref = kv.at[slot(quarter, first, second), quarter]
        target = shifted(quarter, step, 0) if number < 3 else shifted(quarter, 0, step)
        place = quarter * 15 + number
        return remote(ref, ref, send.at[place], recv.at[place], at(*target))

    def start(quarter, number):
        copy(quarter, number, False).start()

    def arrive(quarter, number):
        copy(quarter, number, True).wait_recv()

    tallies[x, y] = counts[...]
    kv[seq] = keyval[...]
    for quarter in range(4):
        for number in (0, 1, 3, 4):
            start(quarter, number)

    def count_copy(axis, shift, incoming):
        number = (0 if axis == 1 else 3) + shift - 1
        if axis == 1:
            ref = tallies.at[x, wrap(y - shift, SIDE) if incoming else y]
            target = at(x, y + shift)
        else:
            ref = tallies.at[wrap(x - shift, SIDE) if incoming else x]
            target = at(x + shift, y)
        return remote(ref, ref, count_send.at[number], count_recv.at[number], target)

    for shift in (1, 2, 3):
        count_copy(1, shift, False).start()

    c1 = HEAD_DIM ** (-0.5) / softcap_limit
    c2 = softcap_limit * math.log2(math.e)
    tile = 256

    def unit(source_x, source_y, diagonal):
        source = source_x * SIDE + source_y
        keys = kv[source, :, :, 0:HEAD_DIM].reshape(SHARD, HEAD_DIM)
        live = live_lanes(tallies[source_x, source_y]).astype(jnp.bfloat16)
        values = jnp.concatenate([kv[source, :, :, HEAD_DIM:].reshape(SHARD, HEAD_DIM), live], axis=1)

        @pl.loop(0, SHARD // tile)
        def _(number):
            first = pl.multiple_of(number * tile, tile)
            scores = lax.dot_general(
                queries[pl.ds(first, tile), :], keys, (((1,), (1,)), ((), ())), preferred_element_type=jnp.float32
            )
            weight = jnp.exp2(c2 * jnp.tanh(scores * c1))
            if diagonal:
                row = lax.broadcasted_iota(jnp.int32, (tile, SHARD), 0) + first
                column = lax.broadcasted_iota(jnp.int32, (tile, SHARD), 1)
                weight = jnp.where(column <= row, weight, 0.0)
            term = jnp.dot(weight.astype(jnp.bfloat16), values, preferred_element_type=jnp.float32)
            if diagonal:
                acc[pl.ds(first, tile), :] = term
            else:
                acc[pl.ds(first, tile), :] += term

    def earlier(dx, dy):
        px, py = wrap(x + dx, SIDE), wrap(y + dy, SIDE)

        @pl.when(px * SIDE + py < seq)
        def _():
            unit(px, py, False)

    unit(x, y, True)
    for shift in (1, 2, 3):
        count_copy(1, shift, True).wait_recv()
    for shift in (1, 2, 3):
        count_copy(0, shift, False).start()
    for quarter in range(4):
        arrive(quarter, 0)
        start(quarter, 2)
        start(quarter, 6)
        start(quarter, 7)
    for quarter in range(4):
        arrive(quarter, 1)
        start(quarter, 9)
        start(quarter, 10)
        arrive(quarter, 3)
        start(quarter, 5)
        arrive(quarter, 4)
    for shift in (1, 2, 3):
        count_copy(0, shift, True).wait_recv()
    earlier(1, 0)
    earlier(-1, 0)
    for quarter in range(4):
        arrive(quarter, 2)
        start(quarter, 12)
        start(quarter, 13)
    earlier(0, 1)
    earlier(0, -1)
    for quarter in range(4):
        arrive(quarter, 6)
        start(quarter, 8)
        arrive(quarter, 9)
        start(quarter, 11)
    for quarter in range(4):
        arrive(quarter, 7)
        arrive(quarter, 10)
        arrive(quarter, 5)
    earlier(1, 1)
    earlier(1, -1)
    for quarter in range(4):
        arrive(quarter, 12)
        start(quarter, 14)
    earlier(-1, 1)
    earlier(-1, -1)
    earlier(2, 0)
    earlier(0, 2)
    for quarter in range(4):
        arrive(quarter, 13)
        arrive(quarter, 8)
        arrive(quarter, 11)
    earlier(2, 1)
    earlier(2, -1)
    earlier(1, 2)
    earlier(-1, 2)
    for quarter in range(4):
        arrive(quarter, 14)
    earlier(2, 2)

    mass = acc[:, HEAD_DIM:]
    attended = (acc[:, 0:HEAD_DIM] / jnp.where(mass > 0, mass, 1.0)).astype(jnp.bfloat16)
    acc[:, 0:HEAD_DIM] = attended.astype(jnp.float32)
    per = SHARD // 16

    @pl.loop(0, 4)
    def _(number):
        rows = acc[pl.ds(pl.multiple_of(number * 4 * per, 4 * per), 4 * per), 0:HEAD_DIM].astype(jnp.bfloat16)
        result = jnp.dot(rows, w_out[...], preferred_element_type=jnp.float32).astype(jnp.bfloat16)
        part[pl.ds(number * 4, 4)] = result.reshape(4, per, WIDTH)

    for shift in (1, 2, 3):
        count_copy(1, shift, False).wait_send()
        count_copy(0, shift, False).wait_send()
    for quarter in range(4):
        for number in range(15):
            copy(quarter, number, False).wait_send()


def mix_kernel(
    part, picked, gains, head, normed, sib, out_buf, in_buf, buf,
    send, recv, sib_send, sib_recv, send2, recv2, sib_send2, sib_recv2,
):
    place = lax.axis_index("exp")
    greet(ring_partners())
    ring_scatter(part, sib, out_buf, in_buf, head, send, recv, sib_send, sib_recv)
    buf[place] = normalize(picked[...].astype(jnp.float32) + head[...], gains[1:2, :])
    ring_gather(buf, send2, recv2, sib_send2, sib_recv2)
    normed[...] = buf[...].reshape(SHARD, WIDTH)


def return_kernel(part, total, sib, out_buf, in_buf, send, recv, sib_send, sib_recv):
    greet(ring_partners())
    ring_scatter(part, sib, out_buf, in_buf, total, send, recv, sib_send, sib_recv)


def dma(count):
    return pltpu.SemaphoreType.DMA((count,))


def params(number, mib=40):
    return pltpu.CompilerParams(collective_id=number, has_side_effects=True, vmem_limit_bytes=mib << 20)


GATHER_SEMS = [dma(16), dma(16), dma(17), dma(17)]
SCATTER_BUFS = [
    pltpu.VMEM((RING, SLOTS, WIDTH), jnp.bfloat16),
    pltpu.VMEM((16, SLOTS, HALF), jnp.bfloat16),
    pltpu.VMEM((16, SLOTS, HALF), jnp.bfloat16),
]
SCATTER_SEMS = [dma(16), dma(16), dma(8), dma(8)]


def local(
    tokens, pick_rows, pick_counts, expert_ids, norm_gains, depth_router,
    w_query, w_keyval, w_out, expert_router, w_expert,
):
    exp_place = lax.axis_index("exp")
    f32, bf16 = jnp.float32, jnp.bfloat16
    matrices = lax.all_gather(w_expert, "seq", axis=3, tiled=True)[0]
    counts = jnp.broadcast_to(pick_counts.astype(f32)[:, None], (16, 128))
    picked, queries, keyval = pl.pallas_call(
        project_kernel,
        out_shape=(
            jax.ShapeDtypeStruct((SLOTS, WIDTH), bf16),
            jax.ShapeDtypeStruct((SHARD, HEAD_DIM), bf16),
            jax.ShapeDtypeStruct((4, QUARTER, 2 * HEAD_DIM), bf16),
        ),
        in_specs=[VMEM] * 6,
        out_specs=(VMEM,) * 3,
        scratch_shapes=[pltpu.VMEM((16, SLOTS, WIDTH), bf16)] + GATHER_SEMS,
        compiler_params=params(0),
        name="project",
    )(tokens, pick_rows, counts, norm_gains, w_query, w_keyval)
    part = pl.pallas_call(
        attend_kernel,
        out_shape=jax.ShapeDtypeStruct((16, SLOTS, WIDTH), bf16),
        in_specs=[VMEM] * 4,
        out_specs=VMEM,
        scratch_shapes=[
            pltpu.VMEM((16, 4, QUARTER, 2 * HEAD_DIM), bf16),
            pltpu.VMEM((SIDE, SIDE, 16, 128), f32),
            pltpu.VMEM((SHARD, 2 * HEAD_DIM), f32),
            dma(60), dma(60), dma(6), dma(6),
        ],
        compiler_params=params(1),
        name="attend",
    )(queries, keyval, counts, w_out)
    head_mine, normed_all = pl.pallas_call(
        mix_kernel,
        out_shape=(
            jax.ShapeDtypeStruct((SLOTS, WIDTH), f32),
            jax.ShapeDtypeStruct((SHARD, WIDTH), bf16),
        ),
        in_specs=[VMEM] * 3,
        out_specs=(VMEM,) * 2,
        scratch_shapes=SCATTER_BUFS + [pltpu.VMEM((16, SLOTS, WIDTH), bf16)] + SCATTER_SEMS + GATHER_SEMS,
        compiler_params=params(2),
        name="mix",
    )(part, picked, norm_gains)

    experts = expert_router.shape[1]
    named = jnp.any(expert_ids == exp_place, axis=1)
    rank = jnp.cumsum(named.astype(jnp.int32)) - 1
    capacity = 416
    select = jnp.where(
        (rank[None, :] == jnp.arange(capacity, dtype=jnp.int32)[:, None]) & named[None, :], 1.0, 0.0
    ).astype(bf16)
    chosen = jnp.any(
        expert_ids[:, :, None] == jnp.arange(experts, dtype=jnp.int32)[None, None, :], axis=1
    )
    scores = jax.nn.sigmoid(jnp.dot(normed_all, expert_router, preferred_element_type=f32))
    scores = jnp.where(chosen, scores, 0.0)
    share = lax.dynamic_index_in_dim(scores, exp_place, 1, keepdims=False) / jnp.sum(scores, axis=1)
    inputs = jnp.dot(select, normed_all, preferred_element_type=f32).astype(bf16)
    gated = jnp.dot(inputs, matrices[0], preferred_element_type=f32)
    upward = jnp.dot(inputs, matrices[1], preferred_element_type=f32)
    hidden = (jax.nn.silu(gated) * upward).astype(bf16)
    result = lax.dot_general(hidden, matrices[2], (((1,), (1,)), ((), ())), preferred_element_type=f32).astype(bf16)
    spread = lax.dot_general(select, result, (((0,), (0,)), ((), ())), preferred_element_type=f32)
    weighted = (spread * share[:, None]).astype(bf16).reshape(16, SLOTS, WIDTH)
    mixture = pl.pallas_call(
        return_kernel,
        out_shape=jax.ShapeDtypeStruct((SLOTS, WIDTH), f32),
        in_specs=[VMEM],
        out_specs=VMEM,
        scratch_shapes=SCATTER_BUFS + SCATTER_SEMS,
        compiler_params=params(3),
        name="bring_back",
    )(weighted)

    my_rows = lax.dynamic_index_in_dim(pick_rows, exp_place, 0, keepdims=False)
    my_count = lax.dynamic_index_in_dim(pick_counts, exp_place, 0, keepdims=False)
    my_valid = jnp.arange(SLOTS, dtype=jnp.int32) < my_count
    delta = jnp.where(my_valid[:, None], head_mine + mixture, 0.0)
    gate = jax.nn.sigmoid(jnp.dot(picked, depth_router, preferred_element_type=f32))
    update = jnp.where(my_valid[:, None], gate[:, None] * delta, 0.0)
    mixed = tokens.astype(f32).at[my_rows].add(update).astype(bf16)
    return (mixed, delta)


def solution(mesh):
    in_specs = (
        P(("seq", "exp"), None), P("seq", None), P("seq"), P("seq", None), P(), P(),
        P(None, "exp"), P(None, None, "exp"), P("exp", None), P(), P("exp", None, None, "seq"),
    )
    out_specs = (P(("seq", "exp"), None), P(("seq", "exp"), None))
    return jax.shard_map(local, mesh=mesh, in_specs=in_specs, out_specs=out_specs, check_vma=False)
```

time: 447 us -> 212 us (0.47)
  waiting for transfers between devices: 247 us -> 1.7 us
  Pallas kernels: 0 us -> 158 us
  blocking collectives: 77.5 us -> 0 us
  matrix products: 64.5 us -> 24.8 us
  local copies, waits for them, and re-layouts: 18.8 us -> 2.24 us
  starting transfers between devices: 8 us -> 0.04 us
  other arithmetic: 16.4 us -> 8.72 us
    pallas_call x0 -> x4, Pallas kernels: none -> 158 us  [the longest x1 61.3 us: local(): pl.pallas_call(attend_kernel, out_shape=jax.ShapeDtypeStruct((16, SLOTS,...]
    all_gather x3 -> x1, waiting for transfers between devices: 147 us -> 1.02 us  [local(): matrices = lax.all_gather(w_expert, 'seq', axis=3, tiled=True)[0]]
    all_to_all x1 -> x0, blocking collectives: 58.9 us -> none  [local(): lax.all_to_all(outgoing, 'exp', split_axis=0, concat_axis=0, tiled=True)]
    reduce_scatter x1 -> x0, waiting for transfers between devices: 53.6 us -> none  [local(): lax.psum_scatter(jnp.dot(attended, w_out, preferred_element_type=jnp.floa...]
    all_to_all x1 -> x0, waiting for transfers between devices: 46.6 us -> none  [local(): lax.all_to_all(served, 'exp', split_axis=0, concat_axis=0, tiled=True)]
    dot_general x9 -> x6, matrix products: 64.5 us -> 24.8 us  [the longest x1 11.9 us: local(): lax.dot_general(hidden, matrices[2], (((1,), (1,)), ((), ())), preferred_...]
    all_gather x1 -> x0, blocking collectives: 18.7 us -> none  [local(): piece_rank = lax.all_gather(key_rank, 'seq', axis=0, tiled=True)]
    reshape x6 -> x0, local copies, waits for them, and re-layouts: 8.33 us -> none  [the longest x1 2.84 us: local(): expert_apply(arrived.reshape(-1, width), w_expert).reshape(arrived.shape)]
  transfers between devices with their start and end apart: 5 -> 1, of which waited for: 5 -> 1; matrix products, arithmetic and copies ran while one was open for 3% -> 5% of each run, Pallas kernels for 0% -> 65%
where the time goes in v1:
time: 212 us; the launch traced here: 210 us
  Pallas kernels  158 us (75%)
  matrix products  24.8 us (12%)
  between operations  14.3 us (7%)
  other arithmetic  8.72 us (4%)
  local copies, waits for them, and re-layouts  2.24 us (1%)
    pallas_call x1, Pallas kernels, local(): pl.pallas_call(attend_kernel, out_shape=jax.ShapeDtypeStruct((16, SLOTS,...  61.3 us
    pallas_call x1, Pallas kernels, local(): pl.pallas_call(mix_kernel, out_shape=(jax.ShapeDtypeStruct((SLOTS, WIDTH)...  45.9 us
    pallas_call x1, Pallas kernels, local(): pl.pallas_call(project_kernel, out_shape=(jax.ShapeDtypeStruct((SLOTS, WI...  29.2 us
    pallas_call x1, Pallas kernels, local(): pl.pallas_call(return_kernel, out_shape=jax.ShapeDtypeStruct((SLOTS, WIDT...  21.8 us
    dot_general x1, matrix products, local(): lax.dot_general(hidden, matrices[2], (((1,), (1,)), ((), ())), preferred_...  11.9 us
    dot_general x1, matrix products, local(): gated = jnp.dot(inputs, matrices[0], preferred_element_type=f32)  6.98 us
  transfers between devices with their start and end apart: 1, of which 1 were waited for; matrix products, arithmetic and copies ran while one was open for 5% of the time, Pallas kernels for 65%

profile of v1, /device:TPU:1, one launch (start us, length us, event | category | flops | bytes accessed | tf_op | source)
XLA Modules:
  0.0 209.9 jit_solution(16839004870174776456)
XLA Ops:
  7.2 0.0 copy-start
  7.2 0.0 copy-start.1
  7.2 0.0 copy-start.5
  7.2 0.0 copy-start.6
  7.2 0.0 copy-start.2
  7.2 0.0 copy-start.3
  7.2 0.0 all-gather.2.cloned.1.call-start
  7.3 0.7 all-gather.2.cloned.1.call-update
  8.0 0.7 convert_element_type.32
  8.7 1.2 dynamic_slice.13
  9.9 0.8 compare_reduce_fusion
  10.7 0.3 reduce-window.9
  11.0 0.1 slice.19
  11.1 0.7 reshape.88
  11.8 0.0 copy-start.4
  11.8 2.9 %convert_element_type.31 = f32[256,2048]{1,0:T(8,128)} convert(bf16[256,2048]{1,0:T(8,128)(2,1)} %tokens.1) | non-fusion elementwise | flops 524288 | bytes 3145728 | tf_op jit(solution)/shard_map/convert_element_type | solution.py:518
  14.6 0.1 broadcast_in_dim.45.counts
  14.7 0.0 copy-done.1
  14.7 0.0 copy-done.5
  14.7 0.0 copy-done.6
  14.7 0.0 copy-done.2
  14.7 0.0 copy-done.3
  14.7 29.2 %project.1 = (bf16[48,2048]{1,0:T(8,128)(2,1)S(1)}, bf16[768,128]{1,0:T(8,128)(2,1)S(1)}, bf16[4,192,256]{2,1,0:T(8,128)(2,1)S(1)}) custom-call(bf16[256,2048]{1,0:T(8,128)(2,1)S(1)} %copy-done.1, s32[16,48]{1,0:T(8,128)S(1)} %copy-done.6, f32[16,128]{1,0:T(8,128)S(1)} %broadcast_in_dim.45.counts, f32[2,2048]{1,0:T(2,128)S(1)} %copy-done.5, ...), custom_call_target="tpu_custom_call" | custom-call | tf_op jit(solution)/shard_map/project/pallas_call | solution.py:442
  44.0 0.0 copy-done.4
  44.0 61.3 %attend.1.part = bf16[16,48,2048]{2,1,0:T(8,128)(2,1)S(1)} custom-call(bf16[768,128]{1,0:T(8,128)(2,1)S(1)} %get-tuple-element.8.queries, bf16[4,192,256]{2,1,0:T(8,128)(2,1)S(1)} %get-tuple-element.9.keyval, f32[16,128]{1,0:T(8,128)S(1)} %broadcast_in_dim.45.counts, bf16[128,2048]{1,0:T(8,128)(2,1)S(1)} %copy-done.4), custom_call_target="tpu_custom_call" | custom-call | tf_op jit(solution)/shard_map/attend/pallas_call | solution.py:455
  105.3 0.0 copy-start.9
  105.3 45.9 %mix.1 = (f32[48,2048]{1,0:T(8,128)S(1)}, bf16[768,2048]{1,0:T(8,128)(2,1)S(1)}) custom-call(bf16[16,48,2048]{2,1,0:T(8,128)(2,1)S(1)} %attend.1.part, bf16[48,2048]{1,0:T(8,128)(2,1)S(1)} %get-tuple-element.7.picked, f32[2,2048]{1,0:T(2,128)S(1)} %copy-done.5), custom_call_target="tpu_custom_call" | custom-call | tf_op jit(solution)/shard_map/mix/pallas_call | solution.py:469
  151.2 0.0 copy-done.9
  151.2 0.0 copy-done
  151.2 1.0 fusion.38
  152.3 0.7 iota_compare_fusion.2
  152.9 0.1 slice_reduce_fusion
  153.0 0.1 add_bitcast_fusion
  153.1 0.2 fusion.15
  153.3 1.5 convolution_convert_fusion
  154.8 1.0 all-gather.2.cloned.1.call-done
  155.8 7.0 %fusion.2 = f32[416,1408]{1,0:T(8,128)} fusion(bf16[416,2048]{1,0:T(8,128)(2,1)S(1)} %convolution_convert_fusion, bf16[1,3,2048,1408]{2,3,1,0:T(8,128)(2,1)} %all-gather.2.cloned.1.call-done), kind=kOutput, calls=%fused_computation.7 | convolution fusion | flops 2399141888 | bytes 9814016 | tf_op jit(solution)/shard_map/dot_general | solution.py:496
  162.8 11.9 %fusion.5 = bf16[416,2048]{1,0:T(8,128)(2,1)} fusion(bf16[1,3,2048,1408]{2,3,1,0:T(8,128)(2,1)} %all-gather.2.cloned.1.call-done, bf16[416,2048]{1,0:T(8,128)(2,1)S(1)} %convolution_convert_fusion, f32[416,1408]{1,0:T(8,128)} %fusion.2), kind=kOutput, calls=%fused_computation.11 | convolution fusion | flops 4802650112 | bytes 17285120 | tf_op jit(solution)/shard_map/dot_general | solution.py:499
  174.7 3.3 %multiply_convert_fusion = bf16[768,2048]{1,0:T(8,128)(2,1)S(1)} fusion(bf16[416,2048]{1,0:T(8,128)(2,1)} %fusion.5, f32[768]{0:T(1024)S(1)} %fusion.31, s32[768]{0:T(1024)S(1)} %add_bitcast_fusion, pred[768]{0:T(1024)(128)(4,1)S(1)} %compare_reduce_fusion), kind=kOutput, calls=%fused_computation.1 | convolution fusion | flops 1313046528 | bytes 4856576 | tf_op jit(solution)/shard_map/dot_general | solution.py:500
  178.0 0.0 copy-start.7
  178.0 21.8 %bring_back.1 = f32[48,2048]{1,0:T(8,128)S(1)} custom-call(bf16[16,48,2048]{2,1,0:T(8,128)(2,1)S(1)} %bitcast.45), custom_call_target="tpu_custom_call" | custom-call | tf_op jit(solution)/shard_map/bring_back/pallas_call | solution.py:502
  199.8 0.1 add_select_fusion
  199.9 0.0 copy-done.7
  199.9 0.0 copy-start.8
  199.9 2.1 scatter_custom_fusion
  202.0 1.1 convert_element_type.40
  203.1 0.0 copy-done.8
  (5 shorter events, 0.1 us)
Async XLA Ops:
  7.2 144.1 %copy-start = (bf16[2048,16]{0,1:T(8,128)(2,1)S(1)}, bf16[2048,16]{0,1:T(8,128)(2,1)}, u32[]{:S(2)}) copy-start(bf16[2048,16]{0,1:T(8,128)(2,1)} %param.20) | copy-start | bytes 196612
  7.2 7.5 %copy-start.1 = (bf16[256,2048]{1,0:T(8,128)(2,1)S(1)}, bf16[256,2048]{1,0:T(8,128)(2,1)}, u32[]{:S(2)}) copy-start(bf16[256,2048]{1,0:T(8,128)(2,1)} %tokens.1) | copy-start | bytes 3145732
  7.2 7.5 %copy-start.5 = (f32[2,2048]{1,0:T(2,128)S(1)}, f32[2,2048]{1,0:T(2,128)}, u32[]{:S(2)}) copy-start(f32[2,2048]{1,0:T(2,128)} %gains.3) | copy-start | bytes 49156
  7.2 7.5 %copy-start.6 = (s32[16,48]{1,0:T(8,128)S(1)}, s32[16,48]{1,0:T(8,128)}, u32[]{:S(2)}) copy-start(s32[16,48]{1,0:T(8,128)} %rows.1) | copy-start | bytes 9220
  7.2 7.5 %copy-start.2 = (bf16[2,2048,128]{2,1,0:T(8,128)(2,1)S(1)}, bf16[2,2048,128]{2,1,0:T(8,128)(2,1)}, u32[]{:S(2)}) copy-start(bf16[2,2048,128]{2,1,0:T(8,128)(2,1)} %w_keyval.1) | copy-start | bytes 3145732
  7.2 7.5 %copy-start.3 = (bf16[2048,128]{1,0:T(8,128)(2,1)S(1)}, bf16[2048,128]{1,0:T(8,128)(2,1)}, u32[]{:S(2)}) copy-start(bf16[2048,128]{1,0:T(8,128)(2,1)} %w_query.1) | copy-start | bytes 1572868
  7.2 148.6 %all-gather.2.cloned.1.call-start = ((), (), s32[]{:S(2)}) async-start(), calls=%async_computation | async-start | bytes 18382848 | tf_op jit(solution)/shard_map/all_gather | solution.py:440
  11.8 32.2 %copy-start.4 = (bf16[128,2048]{1,0:T(8,128)(2,1)S(1)}, bf16[128,2048]{1,0:T(8,128)(2,1)}, u32[]{:S(2)}) copy-start(bf16[128,2048]{1,0:T(8,128)(2,1)} %w_out.1) | copy-start | bytes 1572868
  105.3 45.9 %copy-start.9 = (s32[768,6]{0,1:T(8,128)S(1)}, s32[768,6]{0,1:T(8,128)}, u32[]{:S(2)}) copy-start(s32[768,6]{0,1:T(8,128)} %param.14) | copy-start | bytes 55300
  178.0 21.9 %copy-start.7 = (f32[256,2048]{1,0:T(8,128)S(1)}, f32[256,2048]{1,0:T(8,128)}, u32[]{:S(2)}) copy-start(f32[256,2048]{1,0:T(8,128)} %convert_element_type.31) | copy-start | bytes 6291460
  199.9 3.2 %copy-start.8 = (f32[48,2048]{1,0:T(8,128)}, f32[48,2048]{1,0:T(8,128)S(1)}, u32[]{:S(2)}) copy-start(f32[48,2048]{1,0:T(8,128)S(1)} %add_select_fusion) | copy-start | bytes 1179652
Sparse Core Ops, SparseCore 0:
  10.5 145.2 all-gather.1

commit v2 on v1

v2 whole, which is shorter than its diff:
```python
import functools
import math

import jax
import jax.numpy as jnp
from jax import lax
from jax.experimental import pallas as pl
from jax.experimental.pallas import tpu as pltpu
from jax.sharding import PartitionSpec as P

HEAD_DIM = 128
softcap_limit = 20.0
MESH = pl.DeviceIdType.MESH
SIDE = 4
RING = 8
SLOTS = 48
SHARD = 768
WIDTH = 2048
HALF = 1024
QUARTER = 192
VMEM = pl.BlockSpec(memory_space=pltpu.VMEM)


def wrap(value, size):
    return lax.rem(value + size, size)


def hops(direction, half):
    return 4 if (direction > 0) == (half == 0) else 3


def hop_number(direction, half, hop):
    return ((0 if direction > 0 else 1) * 2 + half) * 4 + hop - 1


def at_exp(index):
    return {"exp": index}


def ring_place():
    place = lax.axis_index("exp")
    return lax.div(place, 2), lax.rem(place, 2)


def greet(partners):
    barrier = pltpu.get_barrier_semaphore()
    for partner in partners:
        pl.semaphore_signal(barrier, inc=1, device_id=partner, device_id_type=MESH)
    pl.semaphore_wait(barrier, len(partners))


def ring_partners():
    z, core = ring_place()
    return [
        at_exp(2 * wrap(z + 1, RING) + core),
        at_exp(2 * wrap(z - 1, RING) + core),
        at_exp(2 * z + 1 - core),
    ]


def remote(src, dst, send, recv, target):
    return pltpu.make_async_remote_copy(
        src_ref=src, dst_ref=dst, send_sem=send, recv_sem=recv, device_id=target, device_id_type=MESH
    )


def ring_gather(buf, send, recv, sib_send, sib_recv):
    z, core = ring_place()
    sibling = at_exp(2 * z + 1 - core)

    def part(origin, side, half):
        return buf.at[2 * origin + side, :, pl.ds(half * HALF, HALF)]

    def hop_copy(direction, half, hop, arriving):
        origin = wrap(z - direction * (hop if arriving else hop - 1), RING)
        ref = part(origin, core, half)
        number = hop_number(direction, half, hop)
        return remote(ref, ref, send.at[number], recv.at[number], at_exp(2 * wrap(z + direction, RING) + core))

    def sib_copy(direction, half, hop, arriving):
        origin = wrap(z - direction * hop, RING)
        ref = part(origin, 1 - core if arriving else core, half)
        number = hop_number(direction, half, hop)
        return remote(ref, ref, sib_send.at[number], sib_recv.at[number], sibling)

    def own_copy(arriving):
        ref = buf.at[2 * z + (1 - core if arriving else core)]
        return remote(ref, ref, sib_send.at[16], sib_recv.at[16], sibling)

    lanes = [(1, 0), (-1, 1), (1, 1), (-1, 0)]
    for direction, half in lanes:
        hop_copy(direction, half, 1, False).start()
    own_copy(False).start()
    for hop in range(1, 5):
        for direction, half in lanes:
            if hop <= hops(direction, half):
                hop_copy(direction, half, hop, True).wait_recv()
                if hop < hops(direction, half):
                    hop_copy(direction, half, hop + 1, False).start()
                sib_copy(direction, half, hop, False).start()
    own_copy(True).wait_recv()
    own_copy(False).wait_send()
    for hop in range(1, 5):
        for direction, half in lanes:
            if hop <= hops(direction, half):
                sib_copy(direction, half, hop, True).wait_recv()
                sib_copy(direction, half, hop, False).wait_send()
                hop_copy(direction, half, hop, False).wait_send()


def ring_scatter(part, sib, out_buf, in_buf, total, send, recv, sib_send, sib_recv):
    z, core = ring_place()
    sibling = at_exp(2 * z + 1 - core)

    def sib_copy(offset):
        target = wrap(z + offset, RING)
        return remote(
            part.at[2 * target + 1 - core], sib.at[target], sib_send.at[offset % RING], sib_recv.at[offset % RING], sibling
        )

    def mine(target, half):
        columns = pl.ds(half * HALF, HALF)
        return part[2 * target + core, :, columns].astype(jnp.float32) + sib[target, :, columns].astype(jnp.float32)

    def hop_copy(direction, half, hop):
        number = hop_number(direction, half, hop)
        return remote(
            out_buf.at[number], in_buf.at[number], send.at[number], recv.at[number],
            at_exp(2 * wrap(z + direction, RING) + core),
        )

    order = [4, 3, -3, 2, -2, 1, -1, 0]
    for offset in order:
        sib_copy(offset).start()
    arrived = set()
    lanes = [(1, 0), (-1, 1), (1, 1), (-1, 0)]

    def have(offset):
        if offset % RING not in arrived:
            arrived.add(offset % RING)
            sib_copy(offset).wait_recv()

    for hop in range(1, 5):
        for direction, half in lanes:
            last = hops(direction, half)
            if hop <= last:
                offset = direction * (last - hop + 1)
                have(offset)
                number = hop_number(direction, half, hop)
                value = mine(wrap(z + offset, RING), half)
                if hop > 1:
                    hop_copy(direction, half, hop - 1).wait_recv()
                    value = value + in_buf[number - 1].astype(jnp.float32)
                out_buf[number] = value.astype(jnp.bfloat16)
                hop_copy(direction, half, hop).start()
    have(0)
    for half in range(2):
        value = mine(z, half)
        for direction in (1, -1):
            last = hops(direction, half)
            hop_copy(direction, half, last).wait_recv()
            value = value + in_buf[hop_number(direction, half, last)].astype(jnp.float32)
        total[:, half * HALF : (half + 1) * HALF] = value
    for offset in order:
        sib_copy(offset).wait_send()
    for direction, half in lanes:
        for hop in range(1, hops(direction, half) + 1):
            hop_copy(direction, half, hop).wait_send()


def normalize(widened, gain):
    scale = lax.rsqrt(jnp.mean(widened * widened, axis=-1, keepdims=True) + 1e-06)
    return (widened * scale * gain).astype(jnp.bfloat16)


def live_lanes(counts):
    row = lax.broadcasted_iota(jnp.int32, (SHARD, 16), 0)
    first = lax.broadcasted_iota(jnp.int32, (SHARD, 16), 1) * SLOTS
    spread = jnp.where((row >= first) & (row < first + SLOTS), 1.0, 0.0).astype(jnp.bfloat16)
    block = lax.broadcasted_iota(jnp.int32, (16, 128), 0).astype(jnp.float32)
    count_of = jnp.dot(spread, counts.astype(jnp.bfloat16), preferred_element_type=jnp.float32)
    block_of = jnp.dot(spread, block.astype(jnp.bfloat16), preferred_element_type=jnp.float32)
    slot = lax.broadcasted_iota(jnp.int32, (SHARD, 128), 0).astype(jnp.float32) - block_of * SLOTS
    return jnp.where(slot < count_of, 1.0, 0.0)


ORDER = [
    (0, 0), (1, 0), (-1, 0), (0, 1), (0, -1), (1, 1), (1, -1), (-1, 1), (-1, -1), (2, 0), (0, 2),
    (2, 1), (2, -1), (1, 2), (-1, 2), (2, 2),
]


def offset_slot(dx, dy):
    return ORDER.index((((dx + 1) % SIDE) - 1, ((dy + 1) % SIDE) - 1))


def torus_place():
    place = lax.axis_index("seq")
    return lax.div(place, SIDE), lax.rem(place, SIDE)


def at_torus(px, py):
    return {"seq": wrap(px, SIDE) * SIDE + wrap(py, SIDE)}


class TorusGather:
    def __init__(self, block, send, recv):
        self.block, self.send, self.recv = block, send, recv
        self.x, self.y = torus_place()

    def copy(self, quarter, number):
        d = 1 if quarter % 2 == 0 else -1
        line, kind = (0, number) if number < 3 else divmod(number - 3, 3)
        step = -d if kind == 1 else d
        along = [-d, d, -2 * d][kind]
        if number < 3:
            origin, move = (along, 0), (step, 0)
        else:
            origin, move = ([0, -d, d, -2 * d][line], along), (0, step)
        source = (origin[0] + move[0], origin[1] + move[1])
        if quarter < 2:
            origin, move, source = origin[::-1], move[::-1], source[::-1]
        place = quarter * 15 + number
        return remote(
            self.block(offset_slot(*source), quarter), self.block(offset_slot(*origin), quarter),
            self.send.at[place], self.recv.at[place], at_torus(self.x + move[0], self.y + move[1]),
        )

    def start(self, quarter, *numbers):
        for number in numbers:
            self.copy(quarter, number).start()

    def arrive(self, *numbers):
        for number in numbers:
            for quarter in range(4):
                self.copy(quarter, number).wait_recv()

    def stage(self, stage):
        for quarter in range(4):
            for needed, following in [
                [(None, (0, 1, 3, 4))],
                [(0, (2, 6, 7)), (1, (9, 10)), (3, (5,))],
                [(2, (12, 13)), (6, (8,)), (9, (11,))],
                [(12, (14,))],
            ][stage]:
                if needed is not None:
                    self.copy(quarter, needed).wait_recv()
                self.start(quarter, *following)

    def finish(self):
        for quarter in range(4):
            for number in range(15):
                self.copy(quarter, number).wait_send()


def block_kernel(
    tokens, rows, counts, ids, gains, w_query, w_keyval, w_out, router, w_expert,
    picked, total,
    gathered, kv, tallies, acc, weights, part, sib, out_buf, in_buf, head, normed, routed, hidden, result,
    sib2, out_buf2, in_buf2,
    g_send, g_recv, gs_send, gs_recv, kv_send, kv_recv, count_send, count_recv, w_send, w_recv,
    r_send, r_recv, rs_send, rs_recv, n_send, n_recv, ns_send, ns_recv, b_send, b_recv, bs_send, bs_recv,
):
    f32, bf16 = jnp.float32, jnp.bfloat16
    place = lax.axis_index("exp")
    seq = lax.axis_index("seq")
    x, y = torus_place()
    greet(
        ring_partners()
        + [at_torus(x + dx, y + dy) for dx, dy in ((0, 1), (0, -1), (0, 2), (1, 0), (-1, 0), (2, 0))]
    )

    weights[0] = w_expert[...]
    w_gather = TorusGather(lambda slot, quarter: weights.at[slot, :, :, pl.ds(quarter * 512, 512)], w_send, w_recv)
    w_gather.stage(0)

    row16 = lax.broadcasted_iota(jnp.int32, (16, 128), 0)
    tally = jnp.zeros((16, 128), f32)
    for device in range(16):
        tally = jnp.where(row16 == device, counts[device].astype(f32), tally)
    tallies[x, y] = tally

    def count_copy(axis, shift):
        number = (0 if axis == 1 else 3) + shift - 1
        if axis == 1:
            ref, target = tallies.at[x, y], at_torus(x, y + shift)
        else:
            ref, target = tallies.at[x], at_torus(x + shift, y)
        return remote(ref, ref, count_send.at[number], count_recv.at[number], target)

    def count_arrival(axis, shift):
        number = (0 if axis == 1 else 3) + shift - 1
        if axis == 1:
            ref, target = tallies.at[x, wrap(y - shift, SIDE)], at_torus(x, y + shift)
        else:
            ref, target = tallies.at[wrap(x - shift, SIDE)], at_torus(x + shift, y)
        return remote(ref, ref, count_send.at[number], count_recv.at[number], target)

    for shift in (1, 2, 3):
        count_copy(1, shift).start()

    mine = rows[pl.ds(place, 1), :]
    onehot = jnp.where(
        lax.broadcasted_iota(jnp.int32, (tokens.shape[0], SLOTS), 0) == mine, 1.0, 0.0
    ).T.astype(bf16)
    chosen = jnp.dot(onehot, tokens[...], preferred_element_type=f32)
    picked[...] = chosen.astype(bf16)
    gathered[place] = normalize(chosen, gains[0:1, :])
    ring_gather(gathered, g_send, g_recv, gs_send, gs_recv)
    for shift in (1, 2, 3):
        count_arrival(1, shift).wait_recv()
    for shift in (1, 2, 3):
        count_copy(0, shift).start()

    inputs = gathered[...].reshape(SHARD, WIDTH)
    keys = jnp.dot(inputs, w_keyval[0], preferred_element_type=f32).astype(bf16)
    values = jnp.dot(inputs, w_keyval[1], preferred_element_type=f32)
    values = (values * live_lanes(tally)).astype(bf16)
    kv[0, :, :, 0:HEAD_DIM] = keys.reshape(4, QUARTER, HEAD_DIM)
    kv[0, :, :, HEAD_DIM:] = values.reshape(4, QUARTER, HEAD_DIM)
    kv_gather = TorusGather(lambda slot, quarter: kv.at[slot, quarter], kv_send, kv_recv)
    kv_gather.stage(0)
    queries = jnp.dot(inputs, w_query[...], preferred_element_type=f32).astype(bf16)

    c1 = HEAD_DIM ** (-0.5) / softcap_limit
    c2 = softcap_limit * math.log2(math.e)
    tile = 256

    def unit(dx, dy):
        diagonal = dx == 0 and dy == 0
        slot = offset_slot(dx, dy)
        unit_keys = kv[slot, :, :, 0:HEAD_DIM].reshape(SHARD, HEAD_DIM)
        live = live_lanes(tallies[wrap(x + dx, SIDE), wrap(y + dy, SIDE)]).astype(bf16)
        unit_values = jnp.concatenate([kv[slot, :, :, HEAD_DIM:].reshape(SHARD, HEAD_DIM), live], axis=1)

        @pl.loop(0, SHARD // tile)
        def _(number):
            first = pl.multiple_of(number * tile, tile)
            scores = lax.dot_general(
                query_ref[pl.ds(first, tile), :], unit_keys, (((1,), (1,)), ((), ())), preferred_element_type=f32
            )
            weight = jnp.exp2(c2 * jnp.tanh(scores * c1))
            if diagonal:
                row = lax.broadcasted_iota(jnp.int32, (tile, SHARD), 0) + first
                column = lax.broadcasted_iota(jnp.int32, (tile, SHARD), 1)
                weight = jnp.where(column <= row, weight, 0.0)
            term = jnp.dot(weight.astype(bf16), unit_values, preferred_element_type=f32)
            if diagonal:
                acc[pl.ds(first, tile), :] = term
            else:
                acc[pl.ds(first, tile), :] += term

    query_ref = hidden.at[0, :, :]
    query_ref[...] = queries

    def earlier(*offsets):
        for dx, dy in offsets:
            px, py = wrap(x + dx, SIDE), wrap(y + dy, SIDE)

            @pl.when(px * SIDE + py < seq)
            def _():
                unit(dx, dy)

    unit(0, 0)
    kv_gather.stage(1)
    kv_gather.arrive(4)
    for shift in (1, 2, 3):
        count_arrival(0, shift).wait_recv()
    earlier((1, 0), (-1, 0))
    kv_gather.stage(2)
    w_gather.stage(1)
    earlier((0, 1), (0, -1))
    kv_gather.stage(3)
    kv_gather.arrive(7, 10, 5)
    earlier((1, 1), (1, -1), (-1, 1), (-1, -1), (2, 0), (0, 2))
    kv_gather.arrive(13, 8, 11)
    earlier((2, 1), (2, -1), (1, 2), (-1, 2))
    kv_gather.arrive(14)
    earlier((2, 2))

    mass = acc[:, HEAD_DIM:]
    query_ref[...] = (acc[:, 0:HEAD_DIM] / jnp.where(mass > 0, mass, 1.0)).astype(bf16)

    @pl.loop(0, 4)
    def _(number):
        block = query_ref[pl.ds(pl.multiple_of(number * 4 * SLOTS, 4 * SLOTS), 4 * SLOTS), :]
        sums = jnp.dot(block, w_out[...], preferred_element_type=f32).astype(bf16)
        part[pl.ds(number * 4, 4)] = sums.reshape(4, SLOTS, WIDTH)

    ring_scatter(part, sib, out_buf, in_buf, head, r_send, r_recv, rs_send, rs_recv)
    w_gather.stage(2)
    normed[place] = normalize(picked[...].astype(f32) + head[...], gains[1:2, :])
    ring_gather(normed, n_send, n_recv, ns_send, ns_recv)
    w_gather.stage(3)

    named_by = jnp.concatenate(
        [
            jnp.max(jnp.where(ids[...] == expert, 1.0, 0.0), axis=0, keepdims=True)
            for expert in range(16)
        ],
        axis=0,
    )
    named = jnp.max(jnp.where(ids[...] == place, 1.0, 0.0), axis=0, keepdims=True)
    before = jnp.where(
        lax.broadcasted_iota(jnp.int32, (SHARD, SHARD), 0) <= lax.broadcasted_iota(jnp.int32, (SHARD, SHARD), 1), 1.0, 0.0
    ).astype(bf16)
    named8 = jnp.broadcast_to(named, (16, SHARD))
    rank = jnp.dot(named8.astype(bf16), before, preferred_element_type=f32) * named8
    rank_column = rank.T[:, 0:1]
    capacity = routed.shape[0]
    select = jnp.where(
        lax.broadcasted_iota(jnp.int32, (capacity, SHARD), 0).astype(f32) + 1.0 == rank[0:1, :], 1.0, 0.0
    ).astype(bf16)
    spread = jnp.where(
        lax.broadcasted_iota(jnp.int32, (SHARD, capacity), 1).astype(f32) + 1.0 == rank_column, 1.0, 0.0
    ).astype(bf16)
    everyone = normed[...].reshape(SHARD, WIDTH)
    routed[...] = jnp.dot(select, everyone, preferred_element_type=f32).astype(bf16)
    scores = lax.dot_general(everyone, router[...], (((1,), (1,)), ((), ())), preferred_element_type=f32)
    scores = named_by.T / (1.0 + jnp.exp(-scores))
    own = jnp.where(lax.broadcasted_iota(jnp.int32, (SHARD, 16), 1) == place, scores, 0.0)
    share = jnp.sum(own, axis=1, keepdims=True) / jnp.sum(scores, axis=1, keepdims=True)

    def experts(first, count):
        @pl.loop(0, count)
        def _(number):
            slot = first + number
            gated = lax.dot_general(
                routed[...], weights[slot, 0], (((1,), (1,)), ((), ())), preferred_element_type=f32
            )
            upward = lax.dot_general(
                routed[...], weights[slot, 1], (((1,), (1,)), ((), ())), preferred_element_type=f32
            )
            units = (gated / (1.0 + jnp.exp(-gated)) * upward).astype(bf16)
            for column in range(4):
                columns = slice(column * 512, column * 512 + 512)
                term = jnp.dot(units, weights[slot, 2, :, columns], preferred_element_type=f32)
                result[:, columns] += term

    result[...] = jnp.zeros_like(result)
    w_gather.arrive(4)
    experts(0, 5)
    w_gather.arrive(7, 10, 5)
    experts(5, 6)
    w_gather.arrive(13, 8, 11)
    experts(11, 4)
    w_gather.arrive(14)
    experts(15, 1)

    for column in range(4):
        columns = slice(column * 512, column * 512 + 512)
        term = jnp.dot(spread, result[:, columns].astype(bf16), preferred_element_type=f32) * share
        part[:, :, columns] = term.astype(bf16).reshape(16, SLOTS, 512)
    ring_scatter(part, sib2, out_buf2, in_buf2, total, b_send, b_recv, bs_send, bs_recv)
    total[...] += head[...]

    for shift in (1, 2, 3):
        count_copy(1, shift).wait_send()
        count_copy(0, shift).wait_send()
    kv_gather.finish()
    w_gather.finish()


def finish_kernel(tokens, rows, counts, picked, total, depth_router, mixed, delta):
    f32, bf16 = jnp.float32, jnp.bfloat16
    place = lax.axis_index("exp")
    live = lax.broadcasted_iota(jnp.int32, (SLOTS, 128), 0) < counts[place]
    live = jnp.where(live, 1.0, 0.0)[:, 0:1] > 0
    change = jnp.where(live, total[...], 0.0)
    delta[...] = change
    logit = jnp.sum(picked[...].astype(f32) * depth_router[...].astype(f32), axis=1, keepdims=True)
    update = change / (1.0 + jnp.exp(-logit))
    high = update.astype(bf16)
    low = (update - high.astype(f32)).astype(bf16)
    onehot = jnp.where(
        lax.broadcasted_iota(jnp.int32, (tokens.shape[0], SLOTS), 0) == rows[pl.ds(place, 1), :], 1.0, 0.0
    ).astype(bf16)
    added = jnp.dot(onehot, high, preferred_element_type=f32) + jnp.dot(onehot, low, preferred_element_type=f32)
    mixed[...] = (tokens[...].astype(f32) + added).astype(bf16)


def dma(count):
    return pltpu.SemaphoreType.DMA((count,))


GATHER_SEMS = [dma(16), dma(16), dma(17), dma(17)]
SCATTER_BUFS = [
    pltpu.VMEM((RING, SLOTS, WIDTH), jnp.bfloat16),
    pltpu.VMEM((16, SLOTS, HALF), jnp.bfloat16),
    pltpu.VMEM((16, SLOTS, HALF), jnp.bfloat16),
]
SCATTER_SEMS = [dma(16), dma(16), dma(8), dma(8)]
SMEM = pl.BlockSpec(memory_space=pltpu.SMEM)
CAPACITY = 416


def local(
    tokens, pick_rows, pick_counts, expert_ids, norm_gains, depth_router,
    w_query, w_keyval, w_out, expert_router, w_expert,
):
    f32, bf16 = jnp.float32, jnp.bfloat16
    units = w_expert.shape[3]
    picked, total = pl.pallas_call(
        block_kernel,
        out_shape=(
            jax.ShapeDtypeStruct((SLOTS, WIDTH), bf16),
            jax.ShapeDtypeStruct((SLOTS, WIDTH), f32),
        ),
        in_specs=[VMEM, VMEM, SMEM] + [VMEM] * 7,
        out_specs=(VMEM,) * 2,
        scratch_shapes=[
            pltpu.VMEM((16, SLOTS, WIDTH), bf16),
            pltpu.VMEM((16, 4, QUARTER, 2 * HEAD_DIM), bf16),
            pltpu.VMEM((SIDE, SIDE, 16, 128), f32),
            pltpu.VMEM((SHARD, 2 * HEAD_DIM), f32),
            pltpu.VMEM((16, 3, units, WIDTH), bf16),
            pltpu.VMEM((16, SLOTS, WIDTH), bf16),
        ]
        + SCATTER_BUFS
        + [
            pltpu.VMEM((SLOTS, WIDTH), f32),
            pltpu.VMEM((16, SLOTS, WIDTH), bf16),
            pltpu.VMEM((CAPACITY, WIDTH), bf16),
            pltpu.VMEM((1, SHARD, HEAD_DIM), bf16),
            pltpu.VMEM((CAPACITY, WIDTH), f32),
        ]
        + SCATTER_BUFS
        + GATHER_SEMS
        + [dma(60), dma(60), dma(6), dma(6), dma(60), dma(60)]
        + SCATTER_SEMS
        + GATHER_SEMS
        + SCATTER_SEMS,
        compiler_params=pltpu.CompilerParams(collective_id=0, has_side_effects=True, vmem_limit_bytes=60 << 20),
        name="block",
    )(
        tokens, pick_rows, pick_counts, expert_ids.T, norm_gains, w_query, w_keyval, w_out,
        expert_router.T, jnp.transpose(w_expert[0], (0, 2, 1)),
    )
    return pl.pallas_call(
        finish_kernel,
        out_shape=(
            jax.ShapeDtypeStruct(tokens.shape, bf16),
            jax.ShapeDtypeStruct((SLOTS, WIDTH), f32),
        ),
        in_specs=[VMEM, VMEM, SMEM] + [VMEM] * 3,
        out_specs=(VMEM,) * 2,
        compiler_params=pltpu.CompilerParams(vmem_limit_bytes=32 << 20),
        name="finish",
    )(tokens, pick_rows, pick_counts, picked, total, depth_router[None, :])


def solution(mesh):
    in_specs = (
        P(("seq", "exp"), None), P("seq", None), P("seq"), P("seq", None), P(), P(),
        P(None, "exp"), P(None, None, "exp"), P("exp", None), P(), P("exp", None, None, "seq"),
    )
    out_specs = (P(("seq", "exp"), None), P(("seq", "exp"), None))
    return jax.shard_map(local, mesh=mesh, in_specs=in_specs, out_specs=out_specs, check_vma=False)
```

time: 212 us -> 207 us (0.976)
  Pallas kernels: 158 us -> 203 us
  matrix products: 24.8 us -> 0 us
  between operations: 14.3 us -> 0.69 us
  other arithmetic: 8.72 us -> 0 us
    pallas_call x4 -> x2, Pallas kernels: 158 us -> 203 us  [the longest x1 201 us: local(): pl.pallas_call(block_kernel, out_shape=(jax.ShapeDtypeStruct((SLOTS, WIDT...]
    dot_general x6 -> x0, matrix products: 24.8 us -> none  [the longest x1 11.9 us: local(): lax.dot_general(hidden, matrices[2], (((1,), (1,)), ((), ())), preferred_...]
    convert_element_type x4 -> x0, other arithmetic: 4.71 us -> none  [the longest x2 3.98 us: local(): mixed = tokens.astype(f32).at[my_rows].add(update).astype(bf16)]
  transfers between devices with their start and end apart: 1 -> 0, of which waited for: 1 -> 0; matrix products, arithmetic and copies ran while one was open for 5% -> 0% of each run, Pallas kernels for 65% -> 0%
where the time goes in v2:
time: 207 us; the launch traced here: 206 us
  Pallas kernels  203 us (98%)
  local copies, waits for them, and re-layouts  2.62 us (1%)
    pallas_call x1, Pallas kernels, local(): pl.pallas_call(block_kernel, out_shape=(jax.ShapeDtypeStruct((SLOTS, WIDT...  201 us

profile of v2, /device:TPU:1, one launch (start us, length us, event | category | flops | bytes accessed | tf_op | source)
XLA Modules:
  0.0 206.5 jit_solution(17584012313645311098)
XLA Ops:
  0.6 0.7 broadcast_in_dim.3.depth_router
  1.3 0.0 copy-start
  1.3 0.0 copy-start.3
  1.3 0.0 copy-start.4
  1.3 200.9 %block.1 = (bf16[48,2048]{1,0:T(8,128)(2,1)}, f32[48,2048]{1,0:T(8,128)}) custom-call(bf16[256,2048]{1,0:T(8,128)(2,1)} %tokens.3, s32[16,48]{1,0:T(8,128)} %rows.3, s32[16]{0:T(128)} %counts.3, s32[6,768]{1,0:T(8,128)} %bitcast.7, f32[2,2048]{1,0:T(2,128)} %gains.1, bf16[2048,128]{1,0:T(8,128)(2,1)} %w_query.1, bf16[2,2048,128]{2,1,0:T(8,128)(2,1)} %w_keyval.1, ...), custom_call_target="tpu_custom_call" | custom-call | tf_op jit(solution)/shard_map/block/pallas_call | solution.py:503
  202.2 0.0 copy-done
  202.2 0.0 copy-done.3
  202.2 0.0 copy-done.4
  202.2 0.0 copy-start.1
  202.2 1.0 copy-done.1
  203.2 0.0 copy-start.2
  203.2 0.9 copy-done.2
  204.2 2.3 %finish.1 = (bf16[256,2048]{1,0:T(8,128)(2,1)}, f32[48,2048]{1,0:T(8,128)}) custom-call(bf16[256,2048]{1,0:T(8,128)(2,1)S(1)} %copy-done, s32[16,48]{1,0:T(8,128)S(1)} %copy-done.3, s32[16]{0:T(128)S(1)} %copy-done.4, bf16[48,2048]{1,0:T(8,128)(2,1)S(1)} %copy-done.2, f32[48,2048]{1,0:T(8,128)S(1)} %copy-done.1, bf16[1,2048]{1,0:T(2,128)(2,1)S(1)} %broadcast_in_dim.3.depth_router), custom_call_target="tpu_custom_call" | custom-call | tf_op jit(solution)/shard_map/finish/pallas_call | solution.py:539
Async XLA Ops:
  1.3 200.9 %copy-start = (bf16[256,2048]{1,0:T(8,128)(2,1)S(1)}, bf16[256,2048]{1,0:T(8,128)(2,1)}, u32[]{:S(2)}) copy-start(bf16[256,2048]{1,0:T(8,128)(2,1)} %tokens.3) | copy-start | bytes 3145732
  1.3 200.9 %copy-start.3 = (s32[16,48]{1,0:T(8,128)S(1)}, s32[16,48]{1,0:T(8,128)}, u32[]{:S(2)}) copy-start(s32[16,48]{1,0:T(8,128)} %rows.3) | copy-start | bytes 9220
  1.3 200.9 %copy-start.4 = (s32[16]{0:T(128)S(1)}, s32[16]{0:T(128)}, u32[]{:S(2)}) copy-start(s32[16]{0:T(128)} %counts.3) | copy-start | bytes 196
  202.2 1.0 copy-start.1
  203.2 0.9 copy-start.2

commit v3 on v2

--- a/solution.py
+++ b/solution.py
@@ -64,7 +64,7 @@
     )
 
 
-def ring_gather(buf, send, recv, sib_send, sib_recv):
+def ring_gather(buf, send, recv, sib_send, sib_recv, between=lambda hop: None):
     z, core = ring_place()
     sibling = at_exp(2 * z + 1 - core)
 
@@ -98,6 +98,7 @@
                 if hop < hops(direction, half):
                     hop_copy(direction, half, hop + 1, False).start()
                 sib_copy(direction, half, hop, False).start()
+        between(hop)
     own_copy(True).wait_recv()
     own_copy(False).wait_send()
     for hop in range(1, 5):
@@ -108,7 +109,7 @@
                 hop_copy(direction, half, hop, False).wait_send()
 
 
-def ring_scatter(part, sib, out_buf, in_buf, total, send, recv, sib_send, sib_recv):
+def ring_scatter(part, sib, out_buf, in_buf, total, send, recv, sib_send, sib_recv, between=lambda hop: None):
     z, core = ring_place()
     sibling = at_exp(2 * z + 1 - core)
 
@@ -153,6 +154,7 @@
                     value = value + in_buf[number - 1].astype(jnp.float32)
                 out_buf[number] = value.astype(jnp.bfloat16)
                 hop_copy(direction, half, hop).start()
+        between(hop)
     have(0)
     for half in range(2):
         value = mine(z, half)
@@ -201,6 +203,11 @@
 
 def at_torus(px, py):
     return {"seq": wrap(px, SIDE) * SIDE + wrap(py, SIDE)}
+
+
+def along(axis, step):
+    x, y = torus_place()
+    return at_torus(x + step, y) if axis == 0 else at_torus(x, y + step)
 
 
 class TorusGather:
@@ -235,8 +242,8 @@
             for quarter in range(4):
                 self.copy(quarter, number).wait_recv()
 
-    def stage(self, stage):
-        for quarter in range(4):
+    def stage(self, stage, quarters=range(4)):
+        for quarter in quarters:
             for needed, following in [
                 [(None, (0, 1, 3, 4))],
                 [(0, (2, 6, 7)), (1, (9, 10)), (3, (5,))],
@@ -253,51 +260,93 @@
                 self.copy(quarter, number).wait_send()
 
 
+class LineGather:
+    def __init__(self, axis, block, send, recv):
+        self.axis, self.block, self.send, self.recv = axis, block, send, recv
+
+    def copy(self, half, number):
+        d = 1 if half == 0 else -1
+        step = -d if number == 1 else d
+        origin = [-d, d, -2 * d][number]
+        place = half * 3 + number
+        return remote(
+            self.block((origin + step) % SIDE, half), self.block(origin % SIDE, half),
+            self.send.at[place], self.recv.at[place], along(self.axis, step),
+        )
+
+    def begin(self):
+        for half in range(2):
+            self.copy(half, 0).start()
+            self.copy(half, 1).start()
+
+    def forward(self):
+        for half in range(2):
+            self.copy(half, 0).wait_recv()
+            self.copy(half, 2).start()
+        for half in range(2):
+            self.copy(half, 1).wait_recv()
+
+    def last(self):
+        for half in range(2):
+            self.copy(half, 2).wait_recv()
+
+    def finish(self):
+        for half in range(2):
+            for number in range(3):
+                self.copy(half, number).wait_send()
+
+
 def block_kernel(
-    tokens, rows, counts, ids, gains, w_query, w_keyval, w_out, router, w_expert,
-    picked, total,
-    gathered, kv, tallies, acc, weights, part, sib, out_buf, in_buf, head, normed, routed, hidden, result,
+    tokens, rows, counts, ids, gains, depth_router, w_query_hbm, w_keyval_hbm, w_out_hbm, router, w_expert,
+    mixed, delta,
+    w_query, w_keyval, w_out, picked, total, gathered, kv, query, tallies, acc, term_out, term_in, mass_out, mass_in,
+    attended, weights, part, sib, out_buf, in_buf, head, normed, routed, units_of, result,
     sib2, out_buf2, in_buf2,
-    g_send, g_recv, gs_send, gs_recv, kv_send, kv_recv, count_send, count_recv, w_send, w_recv,
+    local_sem, g_send, g_recv, gs_send, gs_recv, kv_send, kv_recv, q_send, q_recv, t_send, t_recv, m_send, m_recv,
+    count_send, count_recv, w_send, w_recv,
     r_send, r_recv, rs_send, rs_recv, n_send, n_recv, ns_send, ns_recv, b_send, b_recv, bs_send, bs_recv,
 ):
     f32, bf16 = jnp.float32, jnp.bfloat16
     place = lax.axis_index("exp")
     seq = lax.axis_index("seq")
+    w_units = w_expert.shape[1]
     x, y = torus_place()
+    loads = [
+        pltpu.make_async_copy(source, target, local_sem.at[number])
+        for number, (source, target) in enumerate(
+            ((w_keyval_hbm, w_keyval), (w_query_hbm, w_query), (w_out_hbm, w_out))
+        )
+    ]
+    for load in loads:
+        load.start()
+    weights[0, 0 : w_units] = w_expert[0]
+    weights[0, w_units : 2 * w_units] = w_expert[1]
+    weights[0, 2 * w_units :] = jnp.zeros_like(weights[0, 2 * w_units :])
+    weights[0, 2 * w_units : 3 * w_units] = w_expert[2]
     greet(
         ring_partners()
-        + [at_torus(x + dx, y + dy) for dx, dy in ((0, 1), (0, -1), (0, 2), (1, 0), (-1, 0), (2, 0))]
+        + [at_torus(x + dx, y + dy) for dx, dy in ((0, 1), (0, -1), (0, 2), (1, 0), (-1, 0))]
     )
 
-    weights[0] = w_expert[...]
-    w_gather = TorusGather(lambda slot, quarter: weights.at[slot, :, :, pl.ds(quarter * 512, 512)], w_send, w_recv)
+    w_gather = TorusGather(lambda slot, quarter: weights.at[slot, :, pl.ds(quarter * 512, 512)], w_send, w_recv)
     w_gather.stage(0)
 
     row16 = lax.broadcasted_iota(jnp.int32, (16, 128), 0)
     tally = jnp.zeros((16, 128), f32)
     for device in range(16):
         tally = jnp.where(row16 == device, counts[device].astype(f32), tally)
-    tallies[x, y] = tally
-
-    def count_copy(axis, shift):
-        number = (0 if axis == 1 else 3) + shift - 1
-        if axis == 1:
-            ref, target = tallies.at[x, y], at_torus(x, y + shift)
-        else:
-            ref, target = tallies.at[x], at_torus(x + shift, y)
-        return remote(ref, ref, count_send.at[number], count_recv.at[number], target)
-
-    def count_arrival(axis, shift):
-        number = (0 if axis == 1 else 3) + shift - 1
-        if axis == 1:
-            ref, target = tallies.at[x, wrap(y - shift, SIDE)], at_torus(x, y + shift)
-        else:
-            ref, target = tallies.at[wrap(x - shift, SIDE)], at_torus(x + shift, y)
-        return remote(ref, ref, count_send.at[number], count_recv.at[number], target)
+    tallies[0] = tally
+
+    def count_copy(shift):
+        return remote(
+            tallies.at[0], tallies.at[SIDE - shift], count_send.at[shift - 1], count_recv.at[shift - 1],
+            at_torus(x, y + shift),
+        )
 
     for shift in (1, 2, 3):
-        count_copy(1, shift).start()
+        count_copy(shift).start()
+    acc[...] = jnp.zeros_like(acc)
+    units_of[...] = jnp.zeros_like(units_of)
 
     mine = rows[pl.ds(place, 1), :]
     onehot = jnp.where(
@@ -307,91 +356,144 @@
     picked[...] = chosen.astype(bf16)
     gathered[place] = normalize(chosen, gains[0:1, :])
     ring_gather(gathered, g_send, g_recv, gs_send, gs_recv)
-    for shift in (1, 2, 3):
-        count_arrival(1, shift).wait_recv()
-    for shift in (1, 2, 3):
-        count_copy(0, shift).start()
-
+    for load in loads:
+        load.wait()
+    half_rows = SHARD // 2
     inputs = gathered[...].reshape(SHARD, WIDTH)
     keys = jnp.dot(inputs, w_keyval[0], preferred_element_type=f32).astype(bf16)
     values = jnp.dot(inputs, w_keyval[1], preferred_element_type=f32)
     values = (values * live_lanes(tally)).astype(bf16)
-    kv[0, :, :, 0:HEAD_DIM] = keys.reshape(4, QUARTER, HEAD_DIM)
-    kv[0, :, :, HEAD_DIM:] = values.reshape(4, QUARTER, HEAD_DIM)
-    kv_gather = TorusGather(lambda slot, quarter: kv.at[slot, quarter], kv_send, kv_recv)
-    kv_gather.stage(0)
+    kv[0, :, :, 0:HEAD_DIM] = keys.reshape(2, half_rows, HEAD_DIM)
+    kv[0, :, :, HEAD_DIM:] = values.reshape(2, half_rows, HEAD_DIM)
+    kv_gather = LineGather(1, lambda offset, half: kv.at[offset, half], kv_send, kv_recv)
+    kv_gather.begin()
     queries = jnp.dot(inputs, w_query[...], preferred_element_type=f32).astype(bf16)
+    query[0] = queries.reshape(2, half_rows, HEAD_DIM)
+    q_gather = LineGather(0, lambda offset, half: query.at[offset, half], q_send, q_recv)
+    q_gather.begin()
 
     c1 = HEAD_DIM ** (-0.5) / softcap_limit
     c2 = softcap_limit * math.log2(math.e)
-    tile = 256
-
-    def unit(dx, dy):
-        diagonal = dx == 0 and dy == 0
-        slot = offset_slot(dx, dy)
-        unit_keys = kv[slot, :, :, 0:HEAD_DIM].reshape(SHARD, HEAD_DIM)
-        live = live_lanes(tallies[wrap(x + dx, SIDE), wrap(y + dy, SIDE)]).astype(bf16)
-        unit_values = jnp.concatenate([kv[slot, :, :, HEAD_DIM:].reshape(SHARD, HEAD_DIM), live], axis=1)
-
-        @pl.loop(0, SHARD // tile)
-        def _(number):
-            first = pl.multiple_of(number * tile, tile)
-            scores = lax.dot_general(
-                query_ref[pl.ds(first, tile), :], unit_keys, (((1,), (1,)), ((), ())), preferred_element_type=f32
-            )
-            weight = jnp.exp2(c2 * jnp.tanh(scores * c1))
-            if diagonal:
-                row = lax.broadcasted_iota(jnp.int32, (tile, SHARD), 0) + first
-                column = lax.broadcasted_iota(jnp.int32, (tile, SHARD), 1)
-                weight = jnp.where(column <= row, weight, 0.0)
-            term = jnp.dot(weight.astype(bf16), unit_values, preferred_element_type=f32)
-            if diagonal:
-                acc[pl.ds(first, tile), :] = term
-            else:
-                acc[pl.ds(first, tile), :] += term
-
-    query_ref = hidden.at[0, :, :]
-    query_ref[...] = queries
-
-    def earlier(*offsets):
-        for dx, dy in offsets:
-            px, py = wrap(x + dx, SIDE), wrap(y + dy, SIDE)
-
-            @pl.when(px * SIDE + py < seq)
-            def _():
-                unit(dx, dy)
-
-    unit(0, 0)
-    kv_gather.stage(1)
-    kv_gather.arrive(4)
+    tile = 384
+
+    def unit(dx, dy, diagonal=False):
+        unit_keys = kv[dy, :, :, 0:HEAD_DIM].reshape(SHARD, HEAD_DIM)
+        live = live_lanes(tallies[dy]).astype(bf16)
+        unit_values = jnp.concatenate([kv[dy, :, :, HEAD_DIM:].reshape(SHARD, HEAD_DIM), live], axis=1)
+
+        for half in range(2):
+
+            @pl.loop(0, half_rows // tile)
+            def _(number):
+                first = pl.multiple_of(number * tile, tile)
+                scores = lax.dot_general(
+                    query[dx, half, pl.ds(first, tile), :], unit_keys, (((1,), (1,)), ((), ())),
+                    preferred_element_type=f32,
+                )
+                weight = jnp.exp2(c2 * jnp.tanh(scores * c1))
+                if diagonal:
+                    row = lax.broadcasted_iota(jnp.int32, (tile, SHARD), 0) + first + half * half_rows
+                    column = lax.broadcasted_iota(jnp.int32, (tile, SHARD), 1)
+                    weight = jnp.where(column <= row, weight, 0.0)
+                acc[dx, half, pl.ds(first, tile), :] += jnp.dot(
+                    weight.astype(bf16), unit_values, preferred_element_type=f32
+                )
+
+    def earlier(dx, dy):
+        @pl.when((wrap(x + dx, SIDE) > x) if dx else (wrap(y + dy, SIDE) < y))
+        def _():
+            unit(dx, dy)
+
+    unit(0, 0, True)
+    q_gather.forward()
+    kv_gather.forward()
+    earlier(1, 0)
+    earlier(3, 0)
     for shift in (1, 2, 3):
-        count_arrival(0, shift).wait_recv()
-    earlier((1, 0), (-1, 0))
-    kv_gather.stage(2)
-    w_gather.stage(1)
-    earlier((0, 1), (0, -1))
-    kv_gather.stage(3)
-    kv_gather.arrive(7, 10, 5)
-    earlier((1, 1), (1, -1), (-1, 1), (-1, -1), (2, 0), (0, 2))
-    kv_gather.arrive(13, 8, 11)
-    earlier((2, 1), (2, -1), (1, 2), (-1, 2))
-    kv_gather.arrive(14)
-    earlier((2, 2))
-
-    mass = acc[:, HEAD_DIM:]
-    query_ref[...] = (acc[:, 0:HEAD_DIM] / jnp.where(mass > 0, mass, 1.0)).astype(bf16)
+        count_copy(shift).wait_recv()
+    q_gather.last()
+    w_gather.stage(1, (0,))
+    earlier(2, 0)
+    for dy in (1, 3):
+        for dx in (2, 1, 3, 0):
+            earlier(dx, dy)
+    kv_gather.last()
+    earlier(2, 2)
+
+    def term_copies(direction, half, hop):
+        number = (0 if direction > 0 else 3) + (hop if half == (0 if direction > 0 else 1) else 2)
+        target = along(0, direction)
+        return (
+            remote(term_out.at[number], term_in.at[number], t_send.at[number], t_recv.at[number], target),
+            remote(mass_out.at[number], mass_in.at[number], m_send.at[number], m_recv.at[number], target),
+        ), number
+
+    def send_terms(direction, half, hop, dx, received):
+        copies, number = term_copies(direction, half, hop)
+        value = acc[dx, half, :, 0:HEAD_DIM]
+        mass = acc[dx, half, :, HEAD_DIM:].T[0:8, :]
+        if received is not None:
+            value = value + term_in[received].astype(f32)
+            mass = mass + mass_in[received]
+        term_out[number] = value.astype(bf16)
+        mass_out[number] = mass
+        for copy in copies:
+            copy.start()
+
+    def take_terms(direction, half, hop):
+        copies, number = term_copies(direction, half, hop)
+        for copy in copies:
+            copy.wait_recv()
+        return number
+
+    send_terms(1, 0, 0, 2, None)
+    send_terms(-1, 1, 0, 2, None)
+    earlier(1, 2)
+    earlier(3, 2)
+    send_terms(1, 1, 0, 1, None)
+    send_terms(-1, 0, 0, 3, None)
+    send_terms(1, 0, 1, 1, take_terms(1, 0, 0))
+    send_terms(-1, 1, 1, 3, take_terms(-1, 1, 0))
+    w_gather.stage(1, (1,))
+    earlier(0, 2)
+    for half in range(2):
+        value = acc[0, half, :, 0:HEAD_DIM]
+        mass = acc[0, half, :, HEAD_DIM:]
+        for direction in (-1, 1):
+            number = take_terms(direction, half, 1 if half == (0 if direction > 0 else 1) else 0)
+            value = value + term_in[number].astype(f32)
+            mass = mass + jnp.broadcast_to(mass_in[number].T[:, 0:1], mass.shape)
+        attended[half * half_rows : (half + 1) * half_rows, :] = (
+            value / jnp.where(mass > 0, mass, 1.0)
+        ).astype(bf16)
 
     @pl.loop(0, 4)
     def _(number):
-        block = query_ref[pl.ds(pl.multiple_of(number * 4 * SLOTS, 4 * SLOTS), 4 * SLOTS), :]
+        block = attended[pl.ds(pl.multiple_of(number * 4 * SLOTS, 4 * SLOTS), 4 * SLOTS), :]
         sums = jnp.dot(block, w_out[...], preferred_element_type=f32).astype(bf16)
         part[pl.ds(number * 4, 4)] = sums.reshape(4, SLOTS, WIDTH)
 
-    ring_scatter(part, sib, out_buf, in_buf, head, r_send, r_recv, rs_send, rs_recv)
-    w_gather.stage(2)
+    def during_scatter(hop):
+        if hop == 1:
+            w_gather.stage(1, (2,))
+        if hop == 2:
+            w_gather.stage(1, (3,))
+        if hop == 3:
+            w_gather.stage(2, (0,))
+        if hop == 4:
+            w_gather.stage(2, (1,))
+
+    def during_gather(hop):
+        if hop == 2:
+            w_gather.stage(2, (2,))
+        if hop == 3:
+            w_gather.stage(2, (3,))
+        if hop == 4:
+            w_gather.stage(3)
+
+    ring_scatter(part, sib, out_buf, in_buf, head, r_send, r_recv, rs_send, rs_recv, during_scatter)
     normed[place] = normalize(picked[...].astype(f32) + head[...], gains[1:2, :])
-    ring_gather(normed, n_send, n_recv, ns_send, ns_recv)
-    w_gather.stage(3)
+    ring_gather(normed, n_send, n_recv, ns_send, ns_recv, during_gather)
 
     named_by = jnp.concatenate(
         [
@@ -424,20 +526,35 @@
     def experts(first, count):
         @pl.loop(0, count)
         def _(number):
-            slot = first + number
-            gated = lax.dot_general(
-                routed[...], weights[slot, 0], (((1,), (1,)), ((), ())), preferred_element_type=f32
+            both = lax.dot_general(
+                routed[...], weights[first + number, 0 : 2 * w_units], (((1,), (1,)), ((), ())),
+                preferred_element_type=f32,
             )
-            upward = lax.dot_general(
-                routed[...], weights[slot, 1], (((1,), (1,)), ((), ())), preferred_element_type=f32
+            gated = both[:, 0:w_units]
+            upward = both[:, w_units:]
+            units_of[number, :, 0:w_units] = (gated / (1.0 + jnp.exp(-gated)) * upward).astype(bf16)
+
+        down_rows = 3 * w_units + 8 - 2 * w_units
+
+        @pl.loop(0, 4)
+        def _(number):
+            columns = pl.ds(pl.multiple_of(number * 512, 512), 512)
+            blank = jnp.zeros((128 - down_rows, 512), bf16)
+            left = jnp.concatenate([units_of[chunk] for chunk in range(count)], axis=1)
+            right = jnp.concatenate(
+                [
+                    rows_of
+                    for chunk in range(count)
+                    for rows_of in (weights[first + chunk, 2 * w_units :, columns], blank)
+                ],
+                axis=0,
             )
-            units = (gated / (1.0 + jnp.exp(-gated)) * upward).astype(bf16)
-            for column in range(4):
-                columns = slice(column * 512, column * 512 + 512)
-                term = jnp.dot(units, weights[slot, 2, :, columns], preferred_element_type=f32)
+            term = jnp.dot(left, right, preferred_element_type=f32)
+            if first == 0:
+                result[:, columns] = term
+            else:
                 result[:, columns] += term
 
-    result[...] = jnp.zeros_like(result)
     w_gather.arrive(4)
     experts(0, 5)
     w_gather.arrive(7, 10, 5)
@@ -452,31 +569,27 @@
         term = jnp.dot(spread, result[:, columns].astype(bf16), preferred_element_type=f32) * share
         part[:, :, columns] = term.astype(bf16).reshape(16, SLOTS, 512)
     ring_scatter(part, sib2, out_buf2, in_buf2, total, b_send, b_recv, bs_send, bs_recv)
-    total[...] += head[...]
-
-    for shift in (1, 2, 3):
-        count_copy(1, shift).wait_send()
-        count_copy(0, shift).wait_send()
-    kv_gather.finish()
-    w_gather.finish()
-
-
-def finish_kernel(tokens, rows, counts, picked, total, depth_router, mixed, delta):
-    f32, bf16 = jnp.float32, jnp.bfloat16
-    place = lax.axis_index("exp")
-    live = lax.broadcasted_iota(jnp.int32, (SLOTS, 128), 0) < counts[place]
-    live = jnp.where(live, 1.0, 0.0)[:, 0:1] > 0
-    change = jnp.where(live, total[...], 0.0)
+    live = lax.broadcasted_iota(jnp.int32, (SLOTS, 128), 0).astype(f32) < jnp.max(
+        jnp.where(row16 == place, tally, 0.0), axis=0, keepdims=True
+    )
+    change = jnp.where(jnp.where(live, 1.0, 0.0)[:, 0:1] > 0, total[...] + head[...], 0.0)
     delta[...] = change
     logit = jnp.sum(picked[...].astype(f32) * depth_router[...].astype(f32), axis=1, keepdims=True)
     update = change / (1.0 + jnp.exp(-logit))
     high = update.astype(bf16)
     low = (update - high.astype(f32)).astype(bf16)
-    onehot = jnp.where(
-        lax.broadcasted_iota(jnp.int32, (tokens.shape[0], SLOTS), 0) == rows[pl.ds(place, 1), :], 1.0, 0.0
-    ).astype(bf16)
-    added = jnp.dot(onehot, high, preferred_element_type=f32) + jnp.dot(onehot, low, preferred_element_type=f32)
+    back = jnp.where(lax.broadcasted_iota(jnp.int32, (tokens.shape[0], SLOTS), 0) == mine, 1.0, 0.0).astype(bf16)
+    added = jnp.dot(back, high, preferred_element_type=f32) + jnp.dot(back, low, preferred_element_type=f32)
     mixed[...] = (tokens[...].astype(f32) + added).astype(bf16)
+
+    for shift in (1, 2, 3):
+        count_copy(shift).wait_send()
+    for direction, half, hop in ((1, 0, 0), (1, 0, 1), (1, 1, 0), (-1, 1, 0), (-1, 1, 1), (-1, 0, 0)):
+        for copy in term_copies(direction, half, hop)[0]:
+            copy.wait_send()
+    kv_gather.finish()
+    q_gather.finish()
+    w_gather.finish()
 
 
 def dma(count):
@@ -491,6 +604,7 @@
 ]
 SCATTER_SEMS = [dma(16), dma(16), dma(8), dma(8)]
 SMEM = pl.BlockSpec(memory_space=pltpu.SMEM)
+ANY = pl.BlockSpec(memory_space=pl.ANY)
 CAPACITY = 416
 
 
@@ -500,20 +614,31 @@
 ):
     f32, bf16 = jnp.float32, jnp.bfloat16
     units = w_expert.shape[3]
-    picked, total = pl.pallas_call(
+    return pl.pallas_call(
         block_kernel,
         out_shape=(
-            jax.ShapeDtypeStruct((SLOTS, WIDTH), bf16),
+            jax.ShapeDtypeStruct(tokens.shape, bf16),
             jax.ShapeDtypeStruct((SLOTS, WIDTH), f32),
         ),
-        in_specs=[VMEM, VMEM, SMEM] + [VMEM] * 7,
+        in_specs=[VMEM, VMEM, SMEM] + [VMEM] * 3 + [ANY] * 3 + [VMEM] * 2,
         out_specs=(VMEM,) * 2,
         scratch_shapes=[
+            pltpu.VMEM((WIDTH, HEAD_DIM), bf16),
+            pltpu.VMEM((2, WIDTH, HEAD_DIM), bf16),
+            pltpu.VMEM((HEAD_DIM, WIDTH), bf16),
+            pltpu.VMEM((SLOTS, WIDTH), bf16),
+            pltpu.VMEM((SLOTS, WIDTH), f32),
             pltpu.VMEM((16, SLOTS, WIDTH), bf16),
-            pltpu.VMEM((16, 4, QUARTER, 2 * HEAD_DIM), bf16),
-            pltpu.VMEM((SIDE, SIDE, 16, 128), f32),
-            pltpu.VMEM((SHARD, 2 * HEAD_DIM), f32),
-            pltpu.VMEM((16, 3, units, WIDTH), bf16),
+            pltpu.VMEM((SIDE, 2, SHARD // 2, 2 * HEAD_DIM), bf16),
+            pltpu.VMEM((SIDE, 2, SHARD // 2, HEAD_DIM), bf16),
+            pltpu.VMEM((SIDE, 16, 128), f32),
+            pltpu.VMEM((SIDE, 2, SHARD // 2, 2 * HEAD_DIM), f32),
+            pltpu.VMEM((6, SHARD // 2, HEAD_DIM), bf16),
+            pltpu.VMEM((6, SHARD // 2, HEAD_DIM), bf16),
+            pltpu.VMEM((6, 8, SHARD // 2), f32),
+            pltpu.VMEM((6, 8, SHARD // 2), f32),
+            pltpu.VMEM((SHARD, HEAD_DIM), bf16),
+            pltpu.VMEM((16, 3 * units + 8, WIDTH), bf16),
             pltpu.VMEM((16, SLOTS, WIDTH), bf16),
         ]
         + SCATTER_BUFS
@@ -521,32 +646,23 @@
             pltpu.VMEM((SLOTS, WIDTH), f32),
             pltpu.VMEM((16, SLOTS, WIDTH), bf16),
             pltpu.VMEM((CAPACITY, WIDTH), bf16),
-            pltpu.VMEM((1, SHARD, HEAD_DIM), bf16),
+            pltpu.VMEM((6, CAPACITY, 128), bf16),
             pltpu.VMEM((CAPACITY, WIDTH), f32),
         ]
         + SCATTER_BUFS
+        + [dma(3)]
         + GATHER_SEMS
-        + [dma(60), dma(60), dma(6), dma(6), dma(60), dma(60)]
+        + [dma(6) for _ in range(8)]
+        + [dma(3), dma(3), dma(60), dma(60)]
         + SCATTER_SEMS
         + GATHER_SEMS
         + SCATTER_SEMS,
         compiler_params=pltpu.CompilerParams(collective_id=0, has_side_effects=True, vmem_limit_bytes=60 << 20),
         name="block",
     )(
-        tokens, pick_rows, pick_counts, expert_ids.T, norm_gains, w_query, w_keyval, w_out,
+        tokens, pick_rows, pick_counts, expert_ids.T, norm_gains, depth_router[None, :], w_query, w_keyval, w_out,
         expert_router.T, jnp.transpose(w_expert[0], (0, 2, 1)),
     )
-    return pl.pallas_call(
-        finish_kernel,
-        out_shape=(
-            jax.ShapeDtypeStruct(tokens.shape, bf16),
-            jax.ShapeDtypeStruct((SLOTS, WIDTH), f32),
-        ),
-        in_specs=[VMEM, VMEM, SMEM] + [VMEM] * 3,
-        out_specs=(VMEM,) * 2,
-        compiler_params=pltpu.CompilerParams(vmem_limit_bytes=32 << 20),
-        name="finish",
-    )(tokens, pick_rows, pick_counts, picked, total, depth_router[None, :])
 
 
 def solution(mesh):

time: 207 us -> 175 us (0.85)
  Pallas kernels: 203 us -> 170 us
    pallas_call x2 -> x1, Pallas kernels: 203 us -> 170 us  [local(): pl.pallas_call(block_kernel, out_shape=(jax.ShapeDtypeStruct(tokens.shape...]
where the time goes in v3:
time: 175 us
  Pallas kernels  170 us (97%)
  local copies, waits for them, and re-layouts  4.4 us (3%)
    pallas_call x1, Pallas kernels, local(): pl.pallas_call(block_kernel, out_shape=(jax.ShapeDtypeStruct(tokens.shape...  170 us

profile of v3, /device:TPU:1, one launch (start us, length us, event | category | flops | bytes accessed | tf_op | source)
XLA Modules:
  0.0 175.0 jit_solution(16577364777021634659)
XLA Ops:
  0.6 1.3 broadcast_in_dim.3.depth_router
  1.9 169.9 %block.1 = (bf16[256,2048]{1,0:T(8,128)(2,1)}, f32[48,2048]{1,0:T(8,128)}) custom-call(bf16[256,2048]{1,0:T(8,128)(2,1)} %tokens.1, s32[16,48]{1,0:T(8,128)} %rows.1, s32[16]{0:T(128)} %counts.1, s32[6,768]{1,0:T(8,128)} %bitcast.7, f32[2,2048]{1,0:T(2,128)} %gains.1, bf16[1,2048]{1,0:T(2,128)(2,1)} %broadcast_in_dim.3.depth_router, ...), custom_call_target="tpu_custom_call" | custom-call | tf_op jit(solution)/shard_map/block/pallas_call | solution.py:617
  171.9 0.0 copy-start
  171.9 2.4 %copy.15 = bf16[256,2048]{1,0:T(8,128)(2,1)} copy(bf16[256,2048]{1,0:T(8,128)(2,1)} %get-tuple-element.4) | data formatting | bytes 2097152
  174.2 0.0 copy-done
  174.2 0.7 copy.16
Async XLA Ops:
  171.9 2.4 %copy-start = (f32[48,2048]{1,0:T(8,128)S(1)}, f32[48,2048]{1,0:T(8,128)}, u32[]{:S(2)}) copy-start(f32[48,2048]{1,0:T(8,128)} %get-tuple-element.5) | copy-start | bytes 1179652

commit v4 on v3

--- a/solution.py
+++ b/solution.py
@@ -329,8 +329,8 @@
     )
 
     w_gather = TorusGather(lambda slot, quarter: weights.at[slot, :, pl.ds(quarter * 512, 512)], w_send, w_recv)
-    w_gather.stage(0)
-
+
+    w_gather.stage(0, range(4))
     row16 = lax.broadcasted_iota(jnp.int32, (16, 128), 0)
     tally = jnp.zeros((16, 128), f32)
     for device in range(16):
@@ -405,95 +405,6 @@
             unit(dx, dy)
 
     unit(0, 0, True)
-    q_gather.forward()
-    kv_gather.forward()
-    earlier(1, 0)
-    earlier(3, 0)
-    for shift in (1, 2, 3):
-        count_copy(shift).wait_recv()
-    q_gather.last()
-    w_gather.stage(1, (0,))
-    earlier(2, 0)
-    for dy in (1, 3):
-        for dx in (2, 1, 3, 0):
-            earlier(dx, dy)
-    kv_gather.last()
-    earlier(2, 2)
-
-    def term_copies(direction, half, hop):
-        number = (0 if direction > 0 else 3) + (hop if half == (0 if direction > 0 else 1) else 2)
-        target = along(0, direction)
-        return (
-            remote(term_out.at[number], term_in.at[number], t_send.at[number], t_recv.at[number], target),
-            remote(mass_out.at[number], mass_in.at[number], m_send.at[number], m_recv.at[number], target),
-        ), number
-
-    def send_terms(direction, half, hop, dx, received):
-        copies, number = term_copies(direction, half, hop)
-        value = acc[dx, half, :, 0:HEAD_DIM]
-        mass = acc[dx, half, :, HEAD_DIM:].T[0:8, :]
-        if received is not None:
-            value = value + term_in[received].astype(f32)
-            mass = mass + mass_in[received]
-        term_out[number] = value.astype(bf16)
-        mass_out[number] = mass
-        for copy in copies:
-            copy.start()
-
-    def take_terms(direction, half, hop):
-        copies, number = term_copies(direction, half, hop)
-        for copy in copies:
-            copy.wait_recv()
-        return number
-
-    send_terms(1, 0, 0, 2, None)
-    send_terms(-1, 1, 0, 2, None)
-    earlier(1, 2)
-    earlier(3, 2)
-    send_terms(1, 1, 0, 1, None)
-    send_terms(-1, 0, 0, 3, None)
-    send_terms(1, 0, 1, 1, take_terms(1, 0, 0))
-    send_terms(-1, 1, 1, 3, take_terms(-1, 1, 0))
-    w_gather.stage(1, (1,))
-    earlier(0, 2)
-    for half in range(2):
-        value = acc[0, half, :, 0:HEAD_DIM]
-        mass = acc[0, half, :, HEAD_DIM:]
-        for direction in (-1, 1):
-            number = take_terms(direction, half, 1 if half == (0 if direction > 0 else 1) else 0)
-            value = value + term_in[number].astype(f32)
-            mass = mass + jnp.broadcast_to(mass_in[number].T[:, 0:1], mass.shape)
-        attended[half * half_rows : (half + 1) * half_rows, :] = (
-            value / jnp.where(mass > 0, mass, 1.0)
-        ).astype(bf16)
-
-    @pl.loop(0, 4)
-    def _(number):
-        block = attended[pl.ds(pl.multiple_of(number * 4 * SLOTS, 4 * SLOTS), 4 * SLOTS), :]
-        sums = jnp.dot(block, w_out[...], preferred_element_type=f32).astype(bf16)
-        part[pl.ds(number * 4, 4)] = sums.reshape(4, SLOTS, WIDTH)
-
-    def during_scatter(hop):
-        if hop == 1:
-            w_gather.stage(1, (2,))
-        if hop == 2:
-            w_gather.stage(1, (3,))
-        if hop == 3:
-            w_gather.stage(2, (0,))
-        if hop == 4:
-            w_gather.stage(2, (1,))
-
-    def during_gather(hop):
-        if hop == 2:
-            w_gather.stage(2, (2,))
-        if hop == 3:
-            w_gather.stage(2, (3,))
-        if hop == 4:
-            w_gather.stage(3)
-
-    ring_scatter(part, sib, out_buf, in_buf, head, r_send, r_recv, rs_send, rs_recv, during_scatter)
-    normed[place] = normalize(picked[...].astype(f32) + head[...], gains[1:2, :])
-    ring_gather(normed, n_send, n_recv, ns_send, ns_recv, during_gather)
 
     named_by = jnp.concatenate(
         [
@@ -516,6 +427,89 @@
     spread = jnp.where(
         lax.broadcasted_iota(jnp.int32, (SHARD, capacity), 1).astype(f32) + 1.0 == rank_column, 1.0, 0.0
     ).astype(bf16)
+
+    q_gather.forward()
+    kv_gather.forward()
+    earlier(1, 0)
+    earlier(3, 0)
+    for shift in (1, 2, 3):
+        count_copy(shift).wait_recv()
+    q_gather.last()
+    earlier(2, 0)
+    for dy in (1, 3):
+        for dx in (2, 1, 3, 0):
+            earlier(dx, dy)
+    kv_gather.last()
+    earlier(2, 2)
+
+    def term_copies(direction, half, hop):
+        number = (0 if direction > 0 else 3) + (hop if half == (0 if direction > 0 else 1) else 2)
+        target = along(0, direction)
+        return (
+            remote(term_out.at[number], term_in.at[number], t_send.at[number], t_recv.at[number], target),
+            remote(mass_out.at[number], mass_in.at[number], m_send.at[number], m_recv.at[number], target),
+        ), number
+
+    def send_terms(direction, half, hop, dx, received):
+        copies, number = term_copies(direction, half, hop)
+        value = acc[dx, half, :, 0:HEAD_DIM]
+        mass = acc[dx, half, :, HEAD_DIM:].T[0:8, :]
+        if received is not None:
+            value = value + term_in[received].astype(f32)
+            mass = mass + mass_in[received]
+        term_out[number] = value.astype(bf16)
+        mass_out[number] = mass
+        for copy in copies:
+            copy.start()
+
+    def take_terms(direction, half, hop):
+        copies, number = term_copies(direction, half, hop)
+        for copy in copies:
+            copy.wait_recv()
+        return number
+
+    send_terms(1, 0, 0, 2, None)
+    send_terms(-1, 1, 0, 2, None)
+    earlier(1, 2)
+    earlier(3, 2)
+    send_terms(1, 1, 0, 1, None)
+    send_terms(-1, 0, 0, 3, None)
+    send_terms(1, 0, 1, 1, take_terms(1, 0, 0))
+    send_terms(-1, 1, 1, 3, take_terms(-1, 1, 0))
+    w_gather.stage(1, range(4))
+    earlier(0, 2)
+    for half in range(2):
+        value = acc[0, half, :, 0:HEAD_DIM]
+        mass = acc[0, half, :, HEAD_DIM:]
+        for direction in (-1, 1):
+            number = take_terms(direction, half, 1 if half == (0 if direction > 0 else 1) else 0)
+            value = value + term_in[number].astype(f32)
+            mass = mass + jnp.broadcast_to(mass_in[number].T[:, 0:1], mass.shape)
+        attended[half * half_rows : (half + 1) * half_rows, :] = (
+            value / jnp.where(mass > 0, mass, 1.0)
+        ).astype(bf16)
+
+    @pl.loop(0, 4)
+    def _(number):
+        block = attended[pl.ds(pl.multiple_of(number * 4 * SLOTS, 4 * SLOTS), 4 * SLOTS), :]
+        sums = jnp.dot(block, w_out[...], preferred_element_type=f32).astype(bf16)
+        part[pl.ds(number * 4, 4)] = sums.reshape(4, SLOTS, WIDTH)
+
+    def during_scatter(hop):
+        pass
+
+    def during_gather(hop):
+        if hop == 1:
+            w_gather.stage(2, (0,))
+        if hop == 2:
+            w_gather.stage(2, (2,))
+        if hop == 3:
+            w_gather.stage(2, (1,3))
+
+    ring_scatter(part, sib, out_buf, in_buf, head, r_send, r_recv, rs_send, rs_recv, during_scatter)
+    normed[place] = normalize(picked[...].astype(f32) + head[...], gains[1:2, :])
+    ring_gather(normed, n_send, n_recv, ns_send, ns_recv, during_gather)
+
     everyone = normed[...].reshape(SHARD, WIDTH)
     routed[...] = jnp.dot(select, everyone, preferred_element_type=f32).astype(bf16)
     scores = lax.dot_general(everyone, router[...], (((1,), (1,)), ((), ())), preferred_element_type=f32)
@@ -557,6 +551,7 @@
 
     w_gather.arrive(4)
     experts(0, 5)
+    w_gather.stage(3, range(4))
     w_gather.arrive(7, 10, 5)
     experts(5, 6)
     w_gather.arrive(13, 8, 11)

time: 175 us -> 164 us (0.937)
  Pallas kernels: 170 us -> 159 us
    pallas_call x1, Pallas kernels: 170 us -> 159 us  [local(): pl.pallas_call(block_kernel, out_shape=(jax.ShapeDtypeStruct(tokens.shape...]
where the time goes in v4:
time: 164 us
  Pallas kernels  159 us (97%)
  local copies, waits for them, and re-layouts  4.4 us (3%)
    pallas_call x1, Pallas kernels, local(): pl.pallas_call(block_kernel, out_shape=(jax.ShapeDtypeStruct(tokens.shape...  159 us

profile of v4, /device:TPU:1, one launch (start us, length us, event | category | flops | bytes accessed | tf_op | source)
XLA Modules:
  0.0 164.0 jit_solution(4410009015314598343)
XLA Ops:
  0.6 1.3 broadcast_in_dim.3.depth_router
  1.9 159.0 %block.1 = (bf16[256,2048]{1,0:T(8,128)(2,1)}, f32[48,2048]{1,0:T(8,128)}) custom-call(bf16[256,2048]{1,0:T(8,128)(2,1)} %tokens.1, s32[16,48]{1,0:T(8,128)} %rows.1, s32[16]{0:T(128)} %counts.1, s32[6,768]{1,0:T(8,128)} %bitcast.7, f32[2,2048]{1,0:T(2,128)} %gains.1, bf16[1,2048]{1,0:T(2,128)(2,1)} %broadcast_in_dim.3.depth_router, ...), custom_call_target="tpu_custom_call" | custom-call | tf_op jit(solution)/shard_map/block/pallas_call | solution.py:612
  160.9 0.0 copy-start
  160.9 2.4 %copy.15 = bf16[256,2048]{1,0:T(8,128)(2,1)} copy(bf16[256,2048]{1,0:T(8,128)(2,1)} %get-tuple-element.4) | data formatting | bytes 2097152
  163.2 0.0 copy-done
  163.2 0.7 copy.16
Async XLA Ops:
  160.9 2.4 %copy-start = (f32[48,2048]{1,0:T(8,128)S(1)}, f32[48,2048]{1,0:T(8,128)}, u32[]{:S(2)}) copy-start(f32[48,2048]{1,0:T(8,128)} %get-tuple-element.5) | copy-start | bytes 1179652

commit v5 on v4

--- a/solution.py
+++ b/solution.py
@@ -512,10 +512,6 @@
 
     everyone = normed[...].reshape(SHARD, WIDTH)
     routed[...] = jnp.dot(select, everyone, preferred_element_type=f32).astype(bf16)
-    scores = lax.dot_general(everyone, router[...], (((1,), (1,)), ((), ())), preferred_element_type=f32)
-    scores = named_by.T / (1.0 + jnp.exp(-scores))
-    own = jnp.where(lax.broadcasted_iota(jnp.int32, (SHARD, 16), 1) == place, scores, 0.0)
-    share = jnp.sum(own, axis=1, keepdims=True) / jnp.sum(scores, axis=1, keepdims=True)
 
     def experts(first, count):
         @pl.loop(0, count)
@@ -556,6 +552,10 @@
     experts(5, 6)
     w_gather.arrive(13, 8, 11)
     experts(11, 4)
+    scores = lax.dot_general(everyone, router[...], (((1,), (1,)), ((), ())), preferred_element_type=f32)
+    scores = named_by.T / (1.0 + jnp.exp(-scores))
+    own = jnp.where(lax.broadcasted_iota(jnp.int32, (SHARD, 16), 1) == place, scores, 0.0)
+    share = jnp.sum(own, axis=1, keepdims=True) / jnp.sum(scores, axis=1, keepdims=True)
     w_gather.arrive(14)
     experts(15, 1)
 

time: 164 us -> 166 us (1.012)
  Pallas kernels: 159 us -> 161 us
    pallas_call x1, Pallas kernels: 159 us -> 161 us  [local(): pl.pallas_call(block_kernel, out_shape=(jax.ShapeDtypeStruct(tokens.shape...]
where the time goes in v5:
time: 166 us
  Pallas kernels  161 us (97%)
  local copies, waits for them, and re-layouts  4.4 us (3%)
    pallas_call x1, Pallas kernels, local(): pl.pallas_call(block_kernel, out_shape=(jax.ShapeDtypeStruct(tokens.shape...  161 us

profile of v5, /device:TPU:1, one launch (start us, length us, event | category | flops | bytes accessed | tf_op | source)
XLA Modules:
  0.0 165.9 jit_solution(7675896010607581640)
XLA Ops:
  0.6 1.3 broadcast_in_dim.3.depth_router
  1.9 160.8 %block.1 = (bf16[256,2048]{1,0:T(8,128)(2,1)}, f32[48,2048]{1,0:T(8,128)}) custom-call(bf16[256,2048]{1,0:T(8,128)(2,1)} %tokens.1, s32[16,48]{1,0:T(8,128)} %rows.1, s32[16]{0:T(128)} %counts.1, s32[6,768]{1,0:T(8,128)} %bitcast.7, f32[2,2048]{1,0:T(2,128)} %gains.1, bf16[1,2048]{1,0:T(2,128)(2,1)} %broadcast_in_dim.3.depth_router, ...), custom_call_target="tpu_custom_call" | custom-call | tf_op jit(solution)/shard_map/block/pallas_call | solution.py:612
  162.8 0.0 copy-start
  162.8 2.4 %copy.15 = bf16[256,2048]{1,0:T(8,128)(2,1)} copy(bf16[256,2048]{1,0:T(8,128)(2,1)} %get-tuple-element.4) | data formatting | bytes 2097152
  165.1 0.0 copy-done
  165.1 0.7 copy.16
Async XLA Ops:
  162.8 2.4 %copy-start = (f32[48,2048]{1,0:T(8,128)S(1)}, f32[48,2048]{1,0:T(8,128)}, u32[]{:S(2)}) copy-start(f32[48,2048]{1,0:T(8,128)} %get-tuple-element.5) | copy-start | bytes 1179652
